TPU v7x, 128 devices: a whole 4x4x4 slice. The times are simulated.
128 devices in a mesh: rows: 8 (over z, core), cols: 16 (over y, x).
Axes of the slice: x: 4, y: 4, z: 4, core: 2. Of those that a mesh axis runs over, the one named last changes fastest.
Arguments:
- estimate: float32 [4, 147456], P(None, 'cols'), may hold values from -6 to 6
- dark_hole: int32 [4096], replicated, may hold values from 0 to 147455, as said below
- jacobian: float32 [16384, 18432], P('rows', 'cols'), may hold values from -0.046875 to 0.046875
- basis: float32 [18432, 18432], P('rows', 'cols'), may hold values from -0.046875 to 0.046875
- eigenvalues: float32 [18432], P('rows'), may hold values from 0.5 to 8
- exponents: int32 [8], replicated, may hold values from -2 to 3
- wavelengths: float32 [12], replicated, may hold values from 0.9 to 1.1
- amplitude: float32 [256, 256], replicated, may hold values from 0.2 to 1
- aberration: float32 [256, 256], replicated, may hold values from -3 to 3
- influence: float32 [2, 256, 96], replicated, may hold values from -0.625 to 0.625
Outputs:
- commands: float32 [8, 18432], P(None, 'cols')
- image: float32 [96, 384, 384], P('cols', 'rows')
- contrast: float32 [16, 6], P('cols')
Inputs may be any that keep to these rules, and one draw needn't show every extreme that they name: `dark_hole`: 4096 distinct indices; the first is 0 and the last 147455.
All inputs are finite; a program needn't handle non-finite values.
Results may differ from a plain program's by a relative error of at most 0.0003.
Values sent between devices are 32-bit elements; how exact they have to be, the bound alone decides.
No kernel may reach another device: no remote copies, remote signals or barrier semaphores. Data moves between devices by JAX's collectives and lax.ppermute only.
A program may use at most 64 MiB of HBM per device.

v0:
```python
import math

import jax
import jax.numpy as jnp
from jax import lax
from jax.sharding import PartitionSpec as P

FP = 384


EPSILON = 1e-06
STROKE = 0.05
PIXEL_SCALE = 0.25
TWO_PI = 2.0 * math.pi


def product(left, right):
    return jnp.dot(left, right, precision=lax.Precision.HIGHEST, preferred_element_type=jnp.float32)


def transform_table(positions, wavelength, focal_size, pupil_size):
    freq = (positions - (focal_size / 2 - 0.5)) * (PIXEL_SCALE / wavelength)
    place = (
        jnp.arange(pupil_size, dtype=jnp.int32).astype(jnp.float32) - (pupil_size / 2 - 0.5)
    ) / pupil_size
    angle = -TWO_PI * freq[:, None] * place[None, :]
    return (jnp.cos(angle), jnp.sin(angle))


def dm_surface(command, influence):
    acts = influence.shape[2]
    actuators = command.reshape(2, acts, acts)
    summed = product(product(influence[0], actuators[0]), influence[0].T)
    left_part = product(influence[1], actuators[1])
    return summed + product(left_part, influence[1].T)


def focal_intensity(field_re, field_im, table_y, table_x):
    pupil_size = field_re.shape[1]
    stacked_pupil = jnp.concatenate([field_re, field_im], axis=1)
    upper_part = product(table_y[0], stacked_pupil)
    second = product(table_y[1], stacked_pupil)
    middle_re = upper_part[:, :pupil_size] - second[:, pupil_size:]
    middle_im = upper_part[:, pupil_size:] + second[:, :pupil_size]
    stacked_mid = jnp.concatenate([middle_re, middle_im], axis=0)
    right_side = jnp.concatenate([table_x[0].T, table_x[1].T], axis=1)
    outer_product = product(stacked_mid, right_side)
    rows_count = middle_re.shape[0]
    focal_size = table_x[0].shape[0]
    focal_re = outer_product[:rows_count, :focal_size] - outer_product[rows_count:, focal_size:]
    focal_im = outer_product[:rows_count, focal_size:] + outer_product[rows_count:, :focal_size]
    return focal_re * focal_re + focal_im * focal_im


def on_device(
    estimate,
    dark_hole,
    jacobian,
    basis,
    eigenvalues,
    exponents,
    wavelengths,
    amplitude,
    aberration,
    influence,
):
    row_index = lax.axis_index("rows")
    col_index = lax.axis_index("cols")
    row_count = lax.axis_size("rows")
    col_count = lax.axis_size("cols")
    tile_rows = jacobian.shape[0]
    plane_count = estimate.shape[0]
    per_block = row_count // plane_count
    block_index = row_index // per_block
    offset = row_index % per_block * tile_rows
    picked = lax.dynamic_slice_in_dim(dark_hole, offset, tile_rows)
    gathered = lax.all_gather(estimate, "cols", axis=1, tiled=True)
    one_plane = lax.dynamic_index_in_dim(gathered, block_index, 0, keepdims=False)
    field_rows = jnp.take(one_plane, picked)
    partial_value = product(field_rows[None, :], jacobian)[0]
    gradient = lax.psum(partial_value, "rows")
    modal_part = product(basis, gradient[:, None])[:, 0]
    modal_coeffs = lax.psum(modal_part, "cols")
    damping = jnp.power(2.0, exponents.astype(jnp.float32))
    weights = -modal_coeffs[None, :] / (eigenvalues[None, :] + damping[:, None])
    commands = lax.psum(product(weights, basis), "rows")
    count_cands = commands.shape[0]
    groups_count = col_count // count_cands
    every_command = lax.all_gather(commands, "cols", axis=1, tiled=True)
    chosen = lax.dynamic_index_in_dim(every_command, col_index // groups_count, 0, keepdims=False)
    pupil_size = amplitude.shape[0]
    band_rows = FP // row_count
    per_group = wavelengths.shape[0] // groups_count
    my_waves = lax.dynamic_slice_in_dim(
        wavelengths, col_index % groups_count * per_group, per_group
    )
    height = aberration + 2.0 * STROKE * dm_surface(chosen, influence)
    band_positions = (row_index * band_rows + jnp.arange(band_rows, dtype=jnp.int32)).astype(
        jnp.float32
    )
    full_positions = jnp.arange(FP, dtype=jnp.int32).astype(jnp.float32)

    def check(wavelength):
        phase = TWO_PI / wavelength * height
        table_y = transform_table(band_positions, wavelength, FP, pupil_size)
        table_x = transform_table(full_positions, wavelength, FP, pupil_size)
        return focal_intensity(
            amplitude * jnp.cos(phase), amplitude * jnp.sin(phase), table_y, table_x
        )

    intensity = lax.map(check, my_waves)
    hole_mask = jnp.zeros((FP * FP,), jnp.float32).at[dark_hole].set(1.0)
    band_mask = lax.dynamic_slice_in_dim(
        hole_mask, row_index * band_rows * FP, band_rows * FP
    ).reshape(band_rows, FP)
    hole_part = jnp.sum(intensity * band_mask[None, :, :], axis=(1, 2))
    total_part = jnp.sum(intensity, axis=(1, 2))
    hole_sum, summed = lax.psum((hole_part, total_part), "rows")
    scale = summed / (FP * FP) + EPSILON
    image = intensity / scale[:, None, None]
    contrast = hole_sum / dark_hole.shape[0] / scale
    return (commands, image, contrast[None, :])


def solution(mesh):
    return jax.shard_map(
        on_device,
        mesh=mesh,
        in_specs=(
            P(None, "cols"),
            P(),
            P("rows", "cols"),
            P("rows", "cols"),
            P("rows"),
            P(),
            P(),
            P(),
            P(),
            P(),
        ),
        out_specs=(P(None, "cols"), P("cols", "rows", None), P("cols", None)),
        check_vma=False,
    )
```

profile of v0, /device:TPU:1, one launch (start us, length us, event | category | flops | bytes accessed | tf_op | source)
XLA Modules:
  0.0 293.9 jit_solution(17845318546225732665)
XLA Ops:
  7.2 0.7 all-gather.2.cloned.1.call-update
  8.0 0.7 compare_select_fusion
  8.7 15.7 %scatter_custom_fusion = f32[147456]{0:T(1024)S(1)} fusion(s32[4096]{0:T(1024)S(1)} %compare_select_fusion, f32[4096]{0:T(1024)S(1)} %broadcast.132, f32[]{:T(128)} %constant.151.clone.1), kind=kCustom, calls=%fused_computation.49 | custom fusion | bytes 589828 | tf_op jit(solution)/shard_map/scatter | solution.py:112
  24.5 0.7 dynamic_slice.27
  25.2 0.7 fusion.50
  26.6 31.5 %all-gather.2.cloned.1.call-done = f32[4,147456]{1,0:T(4,128)} async-done(((f32[4,9216]{1,0:T(4,128)}), f32[4,147456]{1,0:T(4,128)}) %all-gather.2.cloned.1.call-update) | async-done | bytes 2359312 | tf_op jit(solution)/shard_map/all_gather | solution.py:77
  58.0 1.9 constant_dynamic-slice_fusion
  59.9 11.8 %gather_fusion = f32[2048]{0:T(1024)S(1)} fusion(f32[147456]{0:T(1024)S(1)} %bitcast.35, s32[2048]{0:T(1024)S(1)} %fusion.50), kind=kCustom, calls=%fused_computation | custom fusion | bytes 24576 | tf_op jit(solution)/shard_map/jit(_take)/gather | solution.py:79
  71.8 7.0 %convolution_reduce_fusion.1 = f32[1152]{0:T(1024)S(1)} fusion(f32[2048,1]{0,1:T(1,128)S(1)} %bitcast.36, f32[2048,1152]{1,0:T(8,128)} %param.14), kind=kOutput, calls=%fused_computation.47 | convolution fusion | flops 28311552 | bytes 9449984 | tf_op jit(solution)/shard_map/dot_general | solution.py:18
  78.8 14.0 %psum.35 = f32[1152]{0:T(1024)S(1)} all-reduce(f32[1152]{0:T(1024)S(1)} %convolution_reduce_fusion.1), channel_id=1, replica_groups=mesh['rows'=8,'cols'=16] {'rows'}, use_global_device_ids=true, to_apply=%region_0.1 | all-reduce | flops 1152 | bytes 9216 | tf_op jit(solution)/shard_map/psum | solution.py:81
  92.8 12.6 %convolution_reduce_fusion = f32[2304]{0:T(1024)S(1)} fusion(f32[1152,1]{0,1:T(1,128)S(1)} %reshape.77, f32[2304,1152]{1,0:T(8,128)} %param.15), kind=kOutput, calls=%fused_computation.46 | convolution fusion | flops 31850496 | bytes 10630656 | tf_op jit(solution)/shard_map/dot_general | solution.py:18
  105.4 58.2 %psum.36 = f32[2304]{0:T(1024)S(1)} all-reduce(f32[2304]{0:T(1024)S(1)} %convolution_reduce_fusion), channel_id=1, replica_groups=mesh['rows'=8,'cols'=16] {'cols'}, use_global_device_ids=true, to_apply=%region_1.2 | all-reduce | flops 2304 | bytes 18432 | tf_op jit(solution)/shard_map/psum | solution.py:83
  163.6 7.6 %fusion.44 = f32[8,1152]{1,0:T(8,128)S(1)} fusion(f32[2304,1152]{1,0:T(8,128)} %param.15, f32[8]{0:T(128)S(1)} %convert_power_fusion, f32[2304]{0:T(1024)S(1)} %copy-done.5, f32[2304]{0:T(1024)S(1)} %neg.4), kind=kOutput, calls=%fused_computation.63 | convolution fusion | flops 254840832 | bytes 10672160 | tf_op jit(solution)/shard_map/dot_general | solution.py:18
  171.2 36.6 %psum.37 = f32[8,1152]{1,0:T(8,128)S(1)} all-reduce(f32[8,1152]{1,0:T(8,128)S(1)} %fusion.44), channel_id=1, replica_groups=mesh['rows'=8,'cols'=16] {'rows'}, use_global_device_ids=true, to_apply=%region_2.3 | all-reduce | flops 9216 | bytes 73728 | tf_op jit(solution)/shard_map/psum | solution.py:86
  207.8 16.4 %all_gather.7 = f32[8,18432]{1,0:T(8,128)S(1)} all-gather(f32[8,1152]{1,0:T(8,128)S(1)} %psum.37), channel_id=1, replica_groups=mesh['rows'=8,'cols'=16] {'cols'}, dimensions={1}, use_global_device_ids=true | all-gather | bytes 626688 | tf_op jit(solution)/shard_map/all_gather | solution.py:89
  226.1 39.5 %while.14 = (s32[]{:T(128)}, f32[6,48,384]{2,1,0:T(8,128)S(1)}, f32[6]{0:T(128)S(1)}, f32[256,256]{1,0:T(8,128)S(1)}, f32[256,256]{1,0:T(8,128)S(1)}, /*index=5*/s32[]{:T(128)}, s32[]{:T(128)}, f32[1]{0:T(128)}, f32[1]{0:T(128)}) while((s32[]{:T(128)}, f32[6,48,384]{2,1,0:T(8,128)S(1)}, f32[6]{0:T(128)S(1)}, ...), condition=%wide.region_4.5_spmd.clone, body=%wide.region_3.4_spmd.clone.sunk | while | flops 378409472 | bytes 4931285 | solution.py:111
  226.1 0.7 dynamic_slice.38
  227.5 1.0 cosine_multiply_fusion.2
  230.6 1.4 multiply_cosine_fusion.6
  232.7 0.7 dynamic_slice.38
  234.1 1.0 cosine_multiply_fusion.2
  237.2 1.4 multiply_cosine_fusion.6
  240.7 1.0 cosine_multiply_fusion.2
  243.8 1.4 multiply_cosine_fusion.6
  247.3 1.0 cosine_multiply_fusion.2
  250.4 1.4 multiply_cosine_fusion.6
  253.8 1.0 cosine_multiply_fusion.2
  256.9 1.4 multiply_cosine_fusion.6
  260.4 1.0 cosine_multiply_fusion.2
  263.5 1.4 multiply_cosine_fusion.6
  265.7 19.9 %all-reduce = (f32[6]{0:T(128)S(1)}, f32[6]{0:T(128)S(1)}) all-reduce(f32[6]{0:T(128)S(1)} %get-tuple-element.135, f32[6]{0:T(128)S(1)} %get-tuple-element.134), channel_id=1, replica_groups=mesh['rows'=8,'cols'=16] {'rows'}, use_global_device_ids=true, to_apply=%region_6.7 | all-reduce | flops 12 | bytes 96 | tf_op jit(solution)/shard_map/psum | solution.py:118
  286.1 0.9 broadcast_divide_fusion
  (82 shorter events, 17.6 us)
Async XLA Ops:
  7.2 64.6 %copy-start.4 = (s32[4096]{0:T(1024)S(1)}, s32[4096]{0:T(1024)}, u32[]{:S(2)}) copy-start(s32[4096]{0:T(1024)} %param.13) | copy-start | bytes 49156
  7.2 50.9 %all-gather.2.cloned.1.call-start = ((), (), s32[]{:S(2)}) async-start(), calls=%async_computation | async-start | bytes 2506752 | tf_op jit(solution)/shard_map/all_gather | solution.py:77
  71.7 91.9 %copy-start.5 = (f32[2304]{0:T(1024)S(1)}, f32[2304]{0:T(1024)}, u32[]{:S(2)}) copy-start(f32[2304]{0:T(1024)} %param.16) | copy-start | bytes 27652
  92.8 131.8 %copy-start.1 = (f32[2,256,96]{1,2,0:T(8,128)S(1)}, f32[2,256,96]{1,2,0:T(8,128)}, u32[]{:S(2)}) copy-start(f32[2,256,96]{1,2,0:T(8,128)} %param.21) | copy-start | bytes 589828
  92.8 132.8 %copy-start.2 = (f32[256,256]{1,0:T(8,128)S(1)}, f32[256,256]{1,0:T(8,128)}, u32[]{:S(2)}) copy-start(f32[256,256]{1,0:T(8,128)} %param.20) | copy-start | bytes 786436
  92.8 133.3 %copy-start = (f32[256,256]{1,0:T(8,128)S(1)}, f32[256,256]{1,0:T(8,128)}, u32[]{:S(2)}) copy-start(f32[256,256]{1,0:T(8,128)} %param.19) | copy-start | bytes 786436
  207.8 18.3 %copy-start.3 = (f32[8,1152]{1,0:T(8,128)}, f32[8,1152]{1,0:T(8,128)S(1)}, u32[]{:S(2)}) copy-start(f32[8,1152]{1,0:T(8,128)S(1)} %psum.37) | copy-start | bytes 110596
Sparse Core Ops, SparseCore 0:
  10.1 47.8 all-gather.1
where the time goes:
time: 294 us
  blocking collectives  145 us (49%)
  matrix products  39.8 us (14%)
  local copies, waits for them, and re-layouts  34.6 us (12%)
  waiting for transfers between devices  32.1 us (11%)
  other arithmetic  18.6 us (6%)
  between operations  14.3 us (5%)
  loops' own time  9.25 us (3%)
    psum x1, blocking collectives, on_device(): modal_coeffs = lax.psum(modal_part, 'cols')  58.2 us
    dot_general x25, matrix products, product(): jnp.dot(left, right, precision=lax.Precision.HIGHEST, preferred_element_t...  39.8 us
    psum x1, blocking collectives, on_device(): commands = lax.psum(product(weights, basis), 'rows')  36.6 us
    all_gather x1, waiting for transfers between devices, on_device(): gathered = lax.all_gather(estimate, 'cols', axis=1, tiled=True)  31.5 us
    psum x1, blocking collectives, on_device(): hole_sum, summed = lax.psum((hole_part, total_part), 'rows')  19.9 us
    all_gather x1, blocking collectives, on_device(): every_command = lax.all_gather(commands, 'cols', axis=1, tiled=True)  16.4 us
    scatter x1, local copies, waits for them, and re-layouts, on_device(): hole_mask = jnp.zeros((FP * FP,), jnp.float32).at[dark_hole].set(1.0)  15.7 us
    psum x1, blocking collectives, on_device(): gradient = lax.psum(partial_value, 'rows')  14 us
  transfers between devices with their start and end apart: 1, of which 1 were waited for; matrix products, arithmetic and copies ran while one was open for 6% of the time, Pallas kernels for 0%

commit v1 on v0

v1 whole, which is shorter than its diff:
```python
import functools

import jax
import jax.numpy as jnp
from jax import lax
from jax.experimental import pallas as pl
from jax.experimental.pallas import tpu as pltpu
from jax.sharding import PartitionSpec as P

FP = 384
PUP = 256
ACT = 96
LANES = 128
EPSILON = 1e-6
STROKE = 0.05
PIXEL_SCALE = 0.25
F32 = jnp.float32
BF16 = jnp.bfloat16
HIGHEST = lax.Precision.HIGHEST

COS = (1.0, -19.73920440673828, 64.93911743164062, -85.45014190673828, 60.16762924194336, -25.967599868774414, 6.528658390045166)
SIN = (6.2831854820251465, -41.34170150756836, 81.60513305664062, -76.70301818847656, 42.02592849731445, -14.899847030639648, 3.2381374835968018)


def horner(coefs, x):
    acc = jnp.full_like(x, coefs[-1])
    for c in coefs[-2::-1]:
        acc = acc * x + c
    return acc


def cos_sin_turns(t):
    r = t - jnp.round(t)
    x = r * r
    return horner(COS, x), horner(SIN, x) * r


def split2(x):
    hi = x.astype(BF16)
    return hi, (x - hi.astype(F32)).astype(BF16)


def mm(a, b):
    return jnp.dot(a, b, preferred_element_type=F32)


def mm_t(a, b, precision=None):
    return lax.dot_general(a, b, (((1,), (1,)), ((), ())), preferred_element_type=F32, precision=precision)


def tdot(a, b):
    return lax.dot_general(a, b, (((0,), (0,)), ((), ())), preferred_element_type=F32)


def spread(ref, row):
    for j in range(ref.shape[0]):
        ref[j] = row


def gathered_sum(ref):
    total = ref[0]
    for j in range(1, ref.shape[0]):
        total = total + ref[j]
    return total


def pick_kernel(est_ref, dh_ref, out_ref, mask_ref, table_ref, flat_ref):
    row = lax.axis_index("rows")
    col = lax.axis_index("cols")
    rows = lax.axis_size("rows")
    planes, width = est_ref.shape
    count = out_ref.shape[-1]
    per_plane = rows // planes
    plane = row // per_plane
    offset = pl.multiple_of((row % per_plane) * count, LANES)
    groups = width // LANES
    ours = lax.broadcasted_iota(jnp.int32, (planes, 1), 0) == plane
    image = jnp.sum(jnp.where(ours, est_ref[...], 0.0), axis=0, keepdims=True)
    for j in range(groups):
        table_ref[j : j + 1, :] = image[:, j * LANES : (j + 1) * LANES]
    table = table_ref[...]
    hi = table.astype(BF16)
    rest = table - hi.astype(F32)
    mid = rest.astype(BF16)
    low = (rest - mid.astype(F32)).astype(BF16)
    index = dh_ref[:, pl.ds(offset, count)]
    place = index - col * width
    group = place >> 7
    lane = place & (LANES - 1)
    one_hot = (lax.broadcasted_iota(jnp.int32, (groups, count), 0) == group).astype(F32).astype(BF16)
    found = tdot(hi, one_hot) + tdot(mid, one_hot) + tdot(low, one_hot)
    keep = lax.broadcasted_iota(jnp.int32, (LANES, count), 0) == lane
    spread(out_ref, jnp.sum(jnp.where(keep, found, 0.0), axis=0, keepdims=True))
    band, full = mask_ref.shape
    per_row = full // LANES
    pix = dh_ref[...] - row * (band * full)
    group = pix >> 7
    lane = pix & (LANES - 1)
    upper = (lax.broadcasted_iota(jnp.int32, (band * per_row, pix.shape[1]), 0) == group).astype(F32).astype(BF16)
    lower = (lax.broadcasted_iota(jnp.int32, (LANES, pix.shape[1]), 0) == lane).astype(F32).astype(BF16)
    flat_ref[...] = mm_t(upper, lower)
    for j in range(per_row):
        mask_ref[:, j * LANES : (j + 1) * LANES] = flat_ref[pl.ds(j, band, stride=per_row), :]


def gradient_kernel(field_ref, jac_ref, out_ref):
    field = gathered_sum(field_ref)
    tile_rows, width = jac_ref.shape
    tiles = width // LANES
    acc = [jnp.zeros((8, LANES), F32) for _ in range(tiles)]
    for b in range(tile_rows // LANES):
        block = jnp.broadcast_to(field[:, b * LANES : (b + 1) * LANES], (LANES, LANES)).T
        for s in range(LANES // 8):
            scale = block[s * 8 : s * 8 + 8]
            at = b * LANES + s * 8
            for l in range(tiles):
                acc[l] = acc[l] + scale * jac_ref[at : at + 8, l * LANES : (l + 1) * LANES]
    row = jnp.concatenate([jnp.sum(a, axis=0, keepdims=True) for a in acc], axis=1)
    spread(out_ref, row)


def modal_kernel(grad_ref, basis_ref, out_ref):
    grad = gathered_sum(grad_ref)
    tile_rows, width = basis_ref.shape
    tiles = width // LANES
    lanes = [jnp.broadcast_to(grad[:, l * LANES : (l + 1) * LANES], (8, LANES)) for l in range(tiles)]
    parts = []
    for b in range(tile_rows // LANES):
        pieces = []
        for s in range(LANES // 8):
            at = b * LANES + s * 8
            acc = lanes[0] * basis_ref[at : at + 8, 0:LANES]
            for l in range(1, tiles):
                acc = acc + lanes[l] * basis_ref[at : at + 8, l * LANES : (l + 1) * LANES]
            pieces.append(acc)
        parts.append(jnp.sum(jnp.concatenate(pieces, axis=0).T, axis=0, keepdims=True))
    spread(out_ref, jnp.concatenate(parts, axis=1))


def command_kernel(modal_ref, eig_ref, exp_ref, basis_ref, out_ref):
    modal = gathered_sum(modal_ref)
    cands = exp_ref.shape[0]
    tile_rows, width = basis_ref.shape
    step = 256
    cand = lax.broadcasted_iota(jnp.int32, (cands, 1), 0)
    power = jnp.zeros((cands, 1), F32)
    for k in range(cands):
        power = jnp.where(cand == k, exp_ref[k].astype(F32), power)
    damping = jnp.exp2(power)
    acc = jnp.zeros((2 * cands, width), F32)
    for b in range(tile_rows // step):
        at = slice(b * step, (b + 1) * step)
        weights = -modal[:, at] / (eig_ref[:, at] + damping)
        high = weights.astype(BF16).astype(F32)
        both = jnp.concatenate([high, weights - high], axis=0).astype(BF16)
        hi, lo = split2(basis_ref[at, :])
        acc = acc + mm(both, hi) + mm(both, lo)
    commands = acc[:cands] + acc[cands:]
    for j in range(out_ref.shape[0]):
        out_ref[j] = commands


def gather_kernel(parts_ref, out_ref, send_ref):
    total = parts_ref[0]
    for j in range(1, parts_ref.shape[0]):
        total = total + parts_ref[j]
    out_ref[...] = total
    copies = send_ref.shape[0] // total.shape[0]
    for j in range(send_ref.shape[0]):
        send_ref[j] = total[j // copies : j // copies + 1]


def check_kernel(cmd_ref, infl_ref, aber_ref, amp_ref, wave_ref, mask_ref, out_ref, stat_ref, act_ref, height_ref, hi_ref, lo_ref):
    row = lax.axis_index("rows")
    col = lax.axis_index("cols")
    waves, band, full = out_ref.shape
    pup = aber_ref.shape[0]
    blocks = cmd_ref.shape[0]
    acts = infl_ref.shape[2]
    mirrors = infl_ref.shape[0]
    groups_count = wave_ref.shape[0] // waves
    first_wave = (col % groups_count) * waves
    per_block = cmd_ref.shape[2] // acts
    per_mirror = blocks // mirrors
    surface = jnp.zeros((pup, pup), F32)
    for m in range(mirrors):
        part = jnp.concatenate([cmd_ref[m * per_mirror + j] for j in range(per_mirror)], axis=0)
        for a in range(per_block):
            act_ref[pl.ds(m * acts + a, per_mirror, stride=per_block), :acts] = part[:, a * acts : (a + 1) * acts]
        actuators = act_ref[m * acts : (m + 1) * acts, :acts]
        right = mm_t(actuators, infl_ref[m], HIGHEST)
        surface = surface + jnp.dot(infl_ref[m], right, precision=HIGHEST, preferred_element_type=F32)
    height_ref[...] = aber_ref[...] + (2.0 * STROKE) * surface
    place = (lax.broadcasted_iota(jnp.int32, (1, pup), 1).astype(F32) - (pup / 2 - 0.5)) * (1.0 / pup)
    near = lax.broadcasted_iota(jnp.int32, (8, 1), 0).astype(F32) - (full / 2 - 0.5)
    far = (lax.broadcasted_iota(jnp.int32, (full // 8, 1), 0) * 8).astype(F32)
    lane = lax.broadcasted_iota(jnp.int32, (1, LANES), 1)
    band_at = pl.multiple_of(row * band, 16)
    mask = mask_ref[...]
    stat = jnp.zeros((1, LANES), F32)
    for w in range(waves):
        inverse = 1.0 / jnp.full((1, LANES), wave_ref[first_wave + w], F32)
        inverse = jnp.concatenate([inverse] * (pup // LANES), axis=1)
        cos, sin = cos_sin_turns(height_ref[...] * inverse)
        amp = amp_ref[...]
        pupil_hi, pupil_lo = split2(jnp.concatenate([amp * cos, amp * sin], axis=1))
        turns = place * (PIXEL_SCALE * inverse)
        near_c, near_s = cos_sin_turns(near * turns)
        far_c, far_s = cos_sin_turns(far * turns)
        for g in range(full // 8):
            fc = far_c[g : g + 1]
            fs = far_s[g : g + 1]
            c = near_c * fc - near_s * fs
            s = -(near_s * fc + near_c * fs)
            rows8 = jnp.concatenate([c, s], axis=1)
            hi = rows8.astype(BF16)
            hi_ref[g * 8 : g * 8 + 8, :] = hi.astype(F32)
            lo_ref[g * 8 : g * 8 + 8, :] = rows8 - hi.astype(F32)
        y_hi = hi_ref[pl.ds(band_at, band), :].astype(BF16)
        y_lo = lo_ref[pl.ds(band_at, band), :].astype(BF16)
        y_hi = jnp.concatenate([y_hi[:, :pup], y_hi[:, pup:]], axis=0)
        y_lo = jnp.concatenate([y_lo[:, :pup], y_lo[:, pup:]], axis=0)
        up = mm(jnp.concatenate([y_hi, y_lo], axis=0), pupil_hi)
        up = up[: 2 * band] + up[2 * band :] + mm(y_hi, pupil_lo)
        mid_re = up[:band, :pup] - up[band:, pup:]
        mid_im = up[:band, pup:] + up[band:, :pup]
        mid_hi, mid_lo = split2(jnp.concatenate([mid_re, mid_im], axis=0))
        both = jnp.concatenate([mid_hi, mid_lo], axis=0)
        outs = []
        for half in range(2):
            x_hi = hi_ref[:, half * pup : (half + 1) * pup].astype(BF16)
            x_lo = lo_ref[:, half * pup : (half + 1) * pup].astype(BF16)
            o = mm_t(both, x_hi)
            outs.append(o[: 2 * band] + o[2 * band :] + mm_t(mid_hi, x_lo))
        re = outs[0][:band] - outs[1][band:]
        im = outs[1][:band] + outs[0][band:]
        intensity = re * re + im * im
        out_ref[w] = intensity
        total = jnp.sum(jnp.sum(intensity, axis=0, keepdims=True), axis=1, keepdims=True)
        hole = jnp.sum(jnp.sum(intensity * mask, axis=0, keepdims=True), axis=1, keepdims=True)
        stat = jnp.where(lane == w, total, stat)
        stat = jnp.where(lane == waves + w, hole, stat)
    spread(stat_ref, stat)


def scale_kernel(stat_ref, int_ref, out_ref, contrast_ref, *, holes):
    waves = int_ref.shape[0]
    stat = gathered_sum(stat_ref)
    scale = stat[:, :waves] / (FP * FP) + EPSILON
    contrast_ref[...] = stat[:, waves : 2 * waves] / holes / scale
    inverse = 1.0 / scale
    for w in range(waves):
        out_ref[w] = int_ref[w] * inverse[:, w : w + 1]


def call(kernel, name, outs, args, scratch=(), smem=(), mib=8):
    specs = [pl.BlockSpec(memory_space=pltpu.SMEM if i in smem else pltpu.VMEM) for i in range(len(args))]
    return pl.pallas_call(
        kernel,
        out_shape=[jax.ShapeDtypeStruct(s, F32) for s in outs],
        in_specs=specs,
        out_specs=[pl.BlockSpec(memory_space=pltpu.VMEM) for _ in outs],
        scratch_shapes=[pltpu.VMEM(s, F32) for s in scratch],
        compiler_params=pltpu.CompilerParams(vmem_limit_bytes=mib << 20),
        name=name,
    )(*args)


def exchange(x, axis):
    return lax.all_to_all(x, axis, 0, 0)


def on_device(estimate, dark_hole, jacobian, basis, eigenvalues, exponents, wavelengths, amplitude, aberration, influence):
    rows = lax.axis_size("rows")
    cols = lax.axis_size("cols")
    tile_rows, width = jacobian.shape
    modes = basis.shape[0]
    cands = exponents.shape[0]
    waves = wavelengths.shape[0] // (cols // cands)
    band = FP // rows
    holes = dark_hole.shape[0]
    groups = estimate.shape[1] // LANES
    share, mask = call(
        pick_kernel, "pick", [(cols, 1, tile_rows), (band, FP)],
        [estimate, dark_hole.reshape(1, holes)],
        scratch=[(groups, LANES), (band * FP // LANES, LANES)],
    )
    share = exchange(share, "cols")
    (grad,) = call(gradient_kernel, "gradient", [(rows, 1, width)], [share, jacobian], mib=14)
    grad = exchange(grad, "rows")
    (modal,) = call(modal_kernel, "modal", [(cols, 1, modes)], [grad, basis], mib=14)
    modal = exchange(modal, "cols")
    (parts,) = call(
        command_kernel, "commands", [(rows, cands, width)],
        [modal, eigenvalues.reshape(1, modes), exponents, basis], smem=(2,), mib=20,
    )
    parts = exchange(parts, "rows")
    commands, chosen = call(gather_kernel, "gather", [(cands, width), (cols, 1, width)], [parts])
    chosen = exchange(chosen, "cols")
    intensity, stat = call(
        check_kernel, "check", [(waves, band, FP), (rows, 1, LANES)],
        [chosen, influence, aberration, amplitude, wavelengths, mask],
        scratch=[(2 * ACT, LANES), (PUP, PUP), (FP, 2 * PUP), (FP, 2 * PUP)], smem=(4,), mib=24,
    )
    stat = exchange(stat, "rows")
    image, contrast = call(
        functools.partial(scale_kernel, holes=holes), "scale", [(waves, band, FP), (1, waves)], [stat, intensity],
    )
    return commands, image, contrast


def solution(mesh):
    return jax.shard_map(
        on_device,
        mesh=mesh,
        in_specs=(
            P(None, "cols"),
            P(),
            P("rows", "cols"),
            P("rows", "cols"),
            P("rows"),
            P(),
            P(),
            P(),
            P(),
            P(),
        ),
        out_specs=(P(None, "cols"), P("cols", "rows", None), P("cols", None)),
        check_vma=False,
    )
```

time: 294 us -> 95.9 us (0.33)
  blocking collectives: 145 us -> 46.4 us
  matrix products: 39.8 us -> 0 us
  local copies, waits for them, and re-layouts: 34.6 us -> 13.5 us
  waiting for transfers between devices: 32.1 us -> 13.2 us
  other arithmetic: 18.6 us -> 0 us
  Pallas kernels: 0 us -> 14.4 us
  between operations: 14.3 us -> 0.73 us
  loops' own time: 9.25 us -> 0 us
  starting transfers between devices: 0.04 us -> 7.02 us
    psum x4 -> x0, blocking collectives: 129 us -> none  [the longest x1 58.2 us: on_device(): modal_coeffs = lax.psum(modal_part, 'cols')]
    all_to_all x0 -> x4, blocking collectives: none -> 46.4 us  [exchange(): return lax.all_to_all(x, axis, 0, 0)]
    dot_general x25 -> x0, matrix products: 39.8 us -> none  [product(): jnp.dot(left, right, precision=lax.Precision.HIGHEST, preferred_element_t...]
    all_gather x1 -> x0, waiting for transfers between devices: 31.5 us -> none  [on_device(): gathered = lax.all_gather(estimate, 'cols', axis=1, tiled=True)]
    all_gather x1 -> x0, blocking collectives: 16.4 us -> none  [on_device(): every_command = lax.all_gather(commands, 'cols', axis=1, tiled=True)]
    scatter x1 -> x0, local copies, waits for them, and re-layouts: 15.7 us -> none  [on_device(): hole_mask = jnp.zeros((FP * FP,), jnp.float32).at[dark_hole].set(1.0)]
    pallas_call x0 -> x7, Pallas kernels: none -> 14.4 us  [call(): pl.pallas_call(kernel, out_shape=[jax.ShapeDtypeStruct(s, F32) for s in o...]
    unnamed x12 -> x23, local copies, waits for them, and re-layouts: 0.04 us -> 13.5 us
  transfers between devices with their start and end apart: 1 -> 2, of which waited for: 1 -> 2; matrix products, arithmetic and copies ran while one was open for 6% -> 0% of each run, Pallas kernels for 0% -> 0%
where the time goes in v1:
time: 95.9 us; the launch traced here: 95.3 us
  blocking collectives  46.4 us (48%)
  Pallas kernels  14.4 us (15%)
  local copies, waits for them, and re-layouts  13.5 us (14%)
  waiting for transfers between devices  13.2 us (14%)
  starting transfers between devices  7.02 us (7%)
    all_to_all x4, blocking collectives, exchange(): return lax.all_to_all(x, axis, 0, 0)  46.4 us
    pallas_call x7, Pallas kernels, call(): pl.pallas_call(kernel, out_shape=[jax.ShapeDtypeStruct(s, F32) for s in o...  14.4 us
    unnamed x23, local copies, waits for them, and re-layouts  13.5 us
    all_to_all x2, waiting for transfers between devices, exchange(): return lax.all_to_all(x, axis, 0, 0)  13.2 us
    all_to_all x2, starting transfers between devices, exchange(): return lax.all_to_all(x, axis, 0, 0)  7.02 us
  transfers between devices with their start and end apart: 2, of which 2 were waited for; matrix products, arithmetic and copies ran while one was open for 0% of the time, Pallas kernels for 0%

profile of v1, /device:TPU:1, one launch (start us, length us, event | category | flops | bytes accessed | tf_op | source)
XLA Modules:
  0.0 95.3 jit_solution(14389885153388736096)
XLA Ops:
  0.6 0.0 copy-start.7
  0.6 0.0 copy-start.5
  0.7 0.9 copy-done.5
  1.6 0.0 copy-start.6
  1.6 0.7 copy-done.6
  2.3 0.0 copy-start.10
  2.3 1.4 %pick.1 = (f32[16,1,2048]{2,1,0:T(1,128)S(1)}, f32[48,384]{1,0:T(8,128)S(1)}) custom-call(f32[4,9216]{1,0:T(4,128)S(1)} %copy-done.5, s32[1,4096]{1,0:T(1,128)S(1)} %bitcast.1), custom_call_target="tpu_custom_call" | custom-call | tf_op jit(solution)/shard_map/pick/pallas_call | solution.py:258
  3.7 14.3 %all_to_all.30.field_ref = f32[16,1,2048]{2,1,0:T(1,128)S(1)} all-to-all(f32[16,1,2048]{2,1,0:T(1,128)S(1)} %get-tuple-element.11), channel_id=1, replica_groups=mesh['rows'=8,'cols'=16] {'cols'}, dimensions={0} | all-to-all | bytes 262144 | tf_op jit(solution)/shard_map/all_to_all | solution.py:270
  17.9 0.0 copy-start.2
  17.9 3.7 %copy-done.2 = f32[2048,1152]{1,0:T(8,128)S(1)} copy-done((f32[2048,1152]{1,0:T(8,128)S(1)}, f32[2048,1152]{1,0:T(8,128)}, u32[]{:S(2)}) %copy-start.2) | copy-done | bytes 9437208
  21.6 0.7 gradient.1
  22.3 11.9 %all_to_all.31.grad_ref = f32[8,1,1152]{2,1,0:T(1,128)S(1)} all-to-all(f32[8,1,1152]{2,1,0:T(1,128)S(1)} %gradient.1), channel_id=1, replica_groups=mesh['rows'=8,'cols'=16] {'rows'}, dimensions={0} | all-to-all | bytes 73728 | tf_op jit(solution)/shard_map/all_to_all | solution.py:270
  34.3 4.0 %copy-done = f32[2304,1152]{1,0:T(8,128)S(1)} copy-done((f32[2304,1152]{1,0:T(8,128)S(1)}, f32[2304,1152]{1,0:T(8,128)}, u32[]{:S(2)}) %copy-start) | copy-done | bytes 10616856
  38.3 1.4 %modal.1 = f32[16,1,2304]{2,1,0:T(1,128)} custom-call(f32[8,1,1152]{2,1,0:T(1,128)S(1)} %all_to_all.31.grad_ref, f32[2304,1152]{1,0:T(8,128)S(1)} %copy-done), custom_call_target="tpu_custom_call" | custom-call | tf_op jit(solution)/shard_map/modal/pallas_call | solution.py:258
  39.7 3.5 %all-to-all-start.2 = ((f32[16,1,2304]{2,1,0:T(1,128)}), f32[16,1,2304]{2,1,0:T(1,128)S(1)}, u32[]{:S(2)}, u32[]{:S(2)}) async-start(f32[16,1,2304]{2,1,0:T(1,128)} %modal.1), calls=%async_computation.2 | async-start | bytes 294912 | tf_op jit(solution)/shard_map/all_to_all | solution.py:270
  43.3 0.0 copy-done.10
  43.3 6.9 %all-to-all-done.2.modal_ref = f32[16,1,2304]{2,1,0:T(1,128)S(1)} async-done(((f32[16,1,2304]{2,1,0:T(1,128)}), f32[16,1,2304]{2,1,0:T(1,128)S(1)}, u32[]{:S(2)}, u32[]{:S(2)}) %all-to-all-start.2) | async-done | bytes 147488 | tf_op jit(solution)/shard_map/all_to_all | solution.py:270
  50.2 0.0 copy-done.7
  50.2 4.0 %copy-done.1 = f32[2304,1152]{1,0:T(8,128)S(1)} copy-done((f32[2304,1152]{1,0:T(8,128)S(1)}, f32[2304,1152]{1,0:T(8,128)}, u32[]{:S(2)}) %copy-start.1) | copy-done | bytes 10616856
  54.2 2.2 %commands.1 = f32[8,8,1152]{2,1,0:T(8,128)S(1)} custom-call(f32[16,1,2304]{2,1,0:T(1,128)S(1)} %all-to-all-done.2.modal_ref, f32[1,2304]{1,0:T(1,128)S(1)} %reshape.13.eig_ref, s32[8]{0:T(128)S(1)} %copy-done.7, f32[2304,1152]{1,0:T(8,128)S(1)} %copy-done.1), custom_call_target="tpu_custom_call" | custom-call | tf_op jit(solution)/shard_map/commands/pallas_call | solution.py:258
  56.4 11.6 %all_to_all.32.parts_ref = f32[8,8,1152]{2,1,0:T(8,128)S(1)} all-to-all(f32[8,8,1152]{2,1,0:T(8,128)S(1)} %commands.1), channel_id=1, replica_groups=mesh['rows'=8,'cols'=16] {'rows'}, dimensions={0} | all-to-all | bytes 589824 | tf_op jit(solution)/shard_map/all_to_all | solution.py:270
  68.0 0.7 gather.1
  68.7 3.5 %all-to-all-start.4 = ((f32[16,1,1152]{2,1,0:T(1,128)}), f32[16,1,1152]{2,1,0:T(1,128)S(1)}, u32[]{:S(2)}, u32[]{:S(2)}) async-start(f32[16,1,1152]{2,1,0:T(1,128)} %get-tuple-element.13), calls=%async_computation.4 | async-start | bytes 147456 | tf_op jit(solution)/shard_map/all_to_all | solution.py:270
  72.2 0.0 copy-done.9
  72.2 0.1 copy.13.infl_ref
  72.3 6.4 %all-to-all-done.4.cmd_ref = f32[16,1,1152]{2,1,0:T(1,128)S(1)} async-done(((f32[16,1,1152]{2,1,0:T(1,128)}), f32[16,1,1152]{2,1,0:T(1,128)S(1)}, u32[]{:S(2)}, u32[]{:S(2)}) %all-to-all-start.4) | async-done | bytes 73760 | tf_op jit(solution)/shard_map/all_to_all | solution.py:270
  78.7 0.0 copy-done.3
  78.7 0.0 copy-done.4
  78.7 0.0 copy-done.8
  78.7 7.1 %check.1 = (f32[6,48,384]{2,1,0:T(8,128)S(1)}, f32[8,1,128]{2,1,0:T(1,128)S(1)}) custom-call(f32[16,1,1152]{2,1,0:T(1,128)S(1)} %all-to-all-done.4.cmd_ref, f32[2,256,96]{2,1,0:T(8,128)S(1)} %copy.13.infl_ref, f32[256,256]{1,0:T(8,128)S(1)} %copy-done.3, f32[256,256]{1,0:T(8,128)S(1)} %copy-done.4, f32[12]{0:T(128)S(1)} %copy-done.8, ...), custom_call_target="tpu_custom_call" | custom-call | tf_op jit(solution)/shard_map/check/pallas_call | solution.py:258
  85.8 8.6 %all_to_all.33.stat_ref = f32[8,1,128]{2,1,0:T(1,128)S(1)} all-to-all(f32[8,1,128]{2,1,0:T(1,128)S(1)} %get-tuple-element.15), channel_id=1, replica_groups=mesh['rows'=8,'cols'=16] {'rows'}, dimensions={0} | all-to-all | bytes 8192 | tf_op jit(solution)/shard_map/all_to_all | solution.py:270
  94.4 0.9 scale.1
  (7 shorter events, 0.0 us)
Async XLA Ops:
  0.6 49.5 %copy-start.7 = (s32[8]{0:T(128)S(1)}, s32[8]{0:T(128)}, u32[]{:S(2)}) copy-start(s32[8]{0:T(128)} %exp_ref.1) | copy-start | bytes 100
  0.6 0.9 copy-start.5
  1.6 0.7 copy-start.6
  2.3 41.0 %copy-start.10 = (f32[2304]{0:T(1024)S(1)}, f32[2304]{0:T(1024)}, u32[]{:S(2)}) copy-start(f32[2304]{0:T(1024)} %param.14) | copy-start | bytes 27652
  17.9 3.7 %copy-start.2 = (f32[2048,1152]{1,0:T(8,128)S(1)}, f32[2048,1152]{1,0:T(8,128)}, u32[]{:S(2)}) copy-start(f32[2048,1152]{1,0:T(8,128)} %jac_ref.1) | copy-start | bytes 28311556
  34.3 4.0 %copy-start = (f32[2304,1152]{1,0:T(8,128)S(1)}, f32[2304,1152]{1,0:T(8,128)}, u32[]{:S(2)}) copy-start(f32[2304,1152]{1,0:T(8,128)} %basis_ref.3) | copy-start | bytes 31850500
  38.3 33.9 %copy-start.9 = (f32[2,256,96]{1,2,0:T(8,128)S(1)}, f32[2,256,96]{1,2,0:T(8,128)}, u32[]{:S(2)}) copy-start(f32[2,256,96]{1,2,0:T(8,128)} %param.19) | copy-start | bytes 589828
  38.3 40.4 %copy-start.3 = (f32[256,256]{1,0:T(8,128)S(1)}, f32[256,256]{1,0:T(8,128)}, u32[]{:S(2)}) copy-start(f32[256,256]{1,0:T(8,128)} %aber_ref.1) | copy-start | bytes 786436
  38.3 40.4 %copy-start.4 = (f32[256,256]{1,0:T(8,128)S(1)}, f32[256,256]{1,0:T(8,128)}, u32[]{:S(2)}) copy-start(f32[256,256]{1,0:T(8,128)} %amp_ref.1) | copy-start | bytes 786436
  38.3 40.4 %copy-start.8 = (f32[12]{0:T(128)S(1)}, f32[12]{0:T(128)}, u32[]{:S(2)}) copy-start(f32[12]{0:T(128)} %wave_ref.1) | copy-start | bytes 148
  39.7 10.4 %all-to-all-start.2 = ((f32[16,1,2304]{2,1,0:T(1,128)}), f32[16,1,2304]{2,1,0:T(1,128)S(1)}, u32[]{:S(2)}, u32[]{:S(2)}) async-start(f32[16,1,2304]{2,1,0:T(1,128)} %modal.1), calls=%async_computation.2 | async-start | bytes 294912 | tf_op jit(solution)/shard_map/all_to_all | solution.py:270
  50.2 4.0 %copy-start.1 = (f32[2304,1152]{1,0:T(8,128)S(1)}, f32[2304,1152]{1,0:T(8,128)}, u32[]{:S(2)}) copy-start(f32[2304,1152]{1,0:T(8,128)} %basis_ref.3) | copy-start | bytes 31850500
  68.7 10.0 %all-to-all-start.4 = ((f32[16,1,1152]{2,1,0:T(1,128)}), f32[16,1,1152]{2,1,0:T(1,128)S(1)}, u32[]{:S(2)}, u32[]{:S(2)}) async-start(f32[16,1,1152]{2,1,0:T(1,128)} %get-tuple-element.13), calls=%async_computation.4 | async-start | bytes 147456 | tf_op jit(solution)/shard_map/all_to_all | solution.py:270

commit v2 on v1

--- a/solution.py
+++ b/solution.py
@@ -64,7 +64,7 @@
     return total
 
 
-def pick_kernel(est_ref, dh_ref, out_ref, mask_ref, table_ref, flat_ref):
+def pick_kernel(est_hbm, dh_hbm, out_ref, est_ref, dh_ref, table_ref, est_sem, dh_sem):
     row = lax.axis_index("rows")
     col = lax.axis_index("cols")
     rows = lax.axis_size("rows")
@@ -73,7 +73,19 @@
     per_plane = rows // planes
     plane = row // per_plane
     offset = pl.multiple_of((row % per_plane) * count, LANES)
+    fetch_dh = pltpu.make_async_copy(dh_hbm, dh_ref, dh_sem)
+    fetch_est = pltpu.make_async_copy(est_hbm, est_ref, est_sem)
+    fetch_dh.start()
+    fetch_est.start()
+    fetch_dh.wait()
     groups = width // LANES
+    index = dh_ref[:, pl.ds(offset, count)]
+    place = index - col * width
+    group = place >> 7
+    lane = place & (LANES - 1)
+    one_hot = (lax.broadcasted_iota(jnp.int32, (groups, count), 0) == group).astype(F32).astype(BF16)
+    keep = lax.broadcasted_iota(jnp.int32, (LANES, count), 0) == lane
+    fetch_est.wait()
     ours = lax.broadcasted_iota(jnp.int32, (planes, 1), 0) == plane
     image = jnp.sum(jnp.where(ours, est_ref[...], 0.0), axis=0, keepdims=True)
     for j in range(groups):
@@ -83,14 +95,12 @@
     rest = table - hi.astype(F32)
     mid = rest.astype(BF16)
     low = (rest - mid.astype(F32)).astype(BF16)
-    index = dh_ref[:, pl.ds(offset, count)]
-    place = index - col * width
-    group = place >> 7
-    lane = place & (LANES - 1)
-    one_hot = (lax.broadcasted_iota(jnp.int32, (groups, count), 0) == group).astype(F32).astype(BF16)
     found = tdot(hi, one_hot) + tdot(mid, one_hot) + tdot(low, one_hot)
-    keep = lax.broadcasted_iota(jnp.int32, (LANES, count), 0) == lane
     spread(out_ref, jnp.sum(jnp.where(keep, found, 0.0), axis=0, keepdims=True))
+
+
+def mask_kernel(dh_ref, mask_ref, flat_ref):
+    row = lax.axis_index("rows")
     band, full = mask_ref.shape
     per_row = full // LANES
     pix = dh_ref[...] - row * (band * full)
@@ -101,6 +111,41 @@
     flat_ref[...] = mm_t(upper, lower)
     for j in range(per_row):
         mask_ref[:, j * LANES : (j + 1) * LANES] = flat_ref[pl.ds(j, band, stride=per_row), :]
+
+
+def wave_inverse(wave_ref, index, width):
+    inverse = 1.0 / jnp.full((1, LANES), wave_ref[index], F32)
+    return jnp.concatenate([inverse] * (width // LANES), axis=1)
+
+
+def first_wave(wave_ref, waves):
+    return (lax.axis_index("cols") % (wave_ref.shape[0] // waves)) * waves
+
+
+def table_kernel(wave_ref, hi_ref, lo_ref):
+    waves, full, width = hi_ref.shape
+    pup = width // 2
+    start = first_wave(wave_ref, waves)
+    place = (lax.broadcasted_iota(jnp.int32, (1, pup), 1).astype(F32) - (pup / 2 - 0.5)) * (1.0 / pup)
+    near = lax.broadcasted_iota(jnp.int32, (8, 1), 0).astype(F32) - (full / 2 - 0.5)
+    far = (lax.broadcasted_iota(jnp.int32, (full // 8, 1), 0) * 8).astype(F32)
+
+    @pl.loop(0, waves)
+    def _(w):
+        turns = place * (PIXEL_SCALE * wave_inverse(wave_ref, start + w, pup))
+        near_c, near_s = cos_sin_turns(near * turns)
+        far_c, far_s = cos_sin_turns(far * turns)
+        for g in range(0, full // 8, 2):
+            rows8 = []
+            for h in (g, g + 1):
+                fc = far_c[h : h + 1]
+                fs = far_s[h : h + 1]
+                c = near_c * fc - near_s * fs
+                s = near_s * fc + near_c * fs
+                rows8.append(jnp.concatenate([c, -s], axis=1))
+            hi, lo = split2(jnp.concatenate(rows8, axis=0))
+            hi_ref[w, g * 8 : g * 8 + 16, :] = hi
+            lo_ref[w, g * 8 : g * 8 + 16, :] = lo
 
 
 def gradient_kernel(field_ref, jac_ref, out_ref):
@@ -160,26 +205,25 @@
         out_ref[j] = commands
 
 
-def gather_kernel(parts_ref, out_ref, send_ref):
-    total = parts_ref[0]
-    for j in range(1, parts_ref.shape[0]):
-        total = total + parts_ref[j]
-    out_ref[...] = total
+def send_kernel(parts_ref, send_ref):
+    total = gathered_sum(parts_ref)
     copies = send_ref.shape[0] // total.shape[0]
     for j in range(send_ref.shape[0]):
         send_ref[j] = total[j // copies : j // copies + 1]
 
 
-def check_kernel(cmd_ref, infl_ref, aber_ref, amp_ref, wave_ref, mask_ref, out_ref, stat_ref, act_ref, height_ref, hi_ref, lo_ref):
+def total_kernel(parts_ref, out_ref):
+    out_ref[...] = gathered_sum(parts_ref)
+
+
+def check_kernel(cmd_ref, infl_ref, aber_ref, amp_ref, wave_ref, mask_ref, hi_ref, lo_ref, out_ref, stat_ref, act_ref, height_ref):
     row = lax.axis_index("rows")
-    col = lax.axis_index("cols")
     waves, band, full = out_ref.shape
     pup = aber_ref.shape[0]
     blocks = cmd_ref.shape[0]
     acts = infl_ref.shape[2]
     mirrors = infl_ref.shape[0]
-    groups_count = wave_ref.shape[0] // waves
-    first_wave = (col % groups_count) * waves
+    start = first_wave(wave_ref, waves)
     per_block = cmd_ref.shape[2] // acts
     per_mirror = blocks // mirrors
     surface = jnp.zeros((pup, pup), F32)
@@ -191,33 +235,16 @@
         right = mm_t(actuators, infl_ref[m], HIGHEST)
         surface = surface + jnp.dot(infl_ref[m], right, precision=HIGHEST, preferred_element_type=F32)
     height_ref[...] = aber_ref[...] + (2.0 * STROKE) * surface
-    place = (lax.broadcasted_iota(jnp.int32, (1, pup), 1).astype(F32) - (pup / 2 - 0.5)) * (1.0 / pup)
-    near = lax.broadcasted_iota(jnp.int32, (8, 1), 0).astype(F32) - (full / 2 - 0.5)
-    far = (lax.broadcasted_iota(jnp.int32, (full // 8, 1), 0) * 8).astype(F32)
     lane = lax.broadcasted_iota(jnp.int32, (1, LANES), 1)
     band_at = pl.multiple_of(row * band, 16)
     mask = mask_ref[...]
     stat = jnp.zeros((1, LANES), F32)
     for w in range(waves):
-        inverse = 1.0 / jnp.full((1, LANES), wave_ref[first_wave + w], F32)
-        inverse = jnp.concatenate([inverse] * (pup // LANES), axis=1)
-        cos, sin = cos_sin_turns(height_ref[...] * inverse)
+        cos, sin = cos_sin_turns(height_ref[...] * wave_inverse(wave_ref, start + w, pup))
         amp = amp_ref[...]
         pupil_hi, pupil_lo = split2(jnp.concatenate([amp * cos, amp * sin], axis=1))
-        turns = place * (PIXEL_SCALE * inverse)
-        near_c, near_s = cos_sin_turns(near * turns)
-        far_c, far_s = cos_sin_turns(far * turns)
-        for g in range(full // 8):
-            fc = far_c[g : g + 1]
-            fs = far_s[g : g + 1]
-            c = near_c * fc - near_s * fs
-            s = -(near_s * fc + near_c * fs)
-            rows8 = jnp.concatenate([c, s], axis=1)
-            hi = rows8.astype(BF16)
-            hi_ref[g * 8 : g * 8 + 8, :] = hi.astype(F32)
-            lo_ref[g * 8 : g * 8 + 8, :] = rows8 - hi.astype(F32)
-        y_hi = hi_ref[pl.ds(band_at, band), :].astype(BF16)
-        y_lo = lo_ref[pl.ds(band_at, band), :].astype(BF16)
+        y_hi = hi_ref[w, pl.ds(band_at, band), :]
+        y_lo = lo_ref[w, pl.ds(band_at, band), :]
         y_hi = jnp.concatenate([y_hi[:, :pup], y_hi[:, pup:]], axis=0)
         y_lo = jnp.concatenate([y_lo[:, :pup], y_lo[:, pup:]], axis=0)
         up = mm(jnp.concatenate([y_hi, y_lo], axis=0), pupil_hi)
@@ -228,10 +255,8 @@
         both = jnp.concatenate([mid_hi, mid_lo], axis=0)
         outs = []
         for half in range(2):
-            x_hi = hi_ref[:, half * pup : (half + 1) * pup].astype(BF16)
-            x_lo = lo_ref[:, half * pup : (half + 1) * pup].astype(BF16)
-            o = mm_t(both, x_hi)
-            outs.append(o[: 2 * band] + o[2 * band :] + mm_t(mid_hi, x_lo))
+            o = mm_t(both, hi_ref[w, :, half * pup : (half + 1) * pup])
+            outs.append(o[: 2 * band] + o[2 * band :] + mm_t(mid_hi, lo_ref[w, :, half * pup : (half + 1) * pup]))
         re = outs[0][:band] - outs[1][band:]
         im = outs[1][:band] + outs[0][band:]
         intensity = re * re + im * im
@@ -253,15 +278,18 @@
         out_ref[w] = int_ref[w] * inverse[:, w : w + 1]
 
 
-def call(kernel, name, outs, args, scratch=(), smem=(), mib=8):
-    specs = [pl.BlockSpec(memory_space=pltpu.SMEM if i in smem else pltpu.VMEM) for i in range(len(args))]
+def call(kernel, name, outs, args, scratch=(), smem=(), hbm=(), mib=16, cost=2e10):
+    def space(i):
+        return pltpu.SMEM if i in smem else pltpu.HBM if i in hbm else pltpu.VMEM
+
     return pl.pallas_call(
         kernel,
-        out_shape=[jax.ShapeDtypeStruct(s, F32) for s in outs],
-        in_specs=specs,
+        out_shape=[s if isinstance(s, jax.ShapeDtypeStruct) else jax.ShapeDtypeStruct(s, F32) for s in outs],
+        in_specs=[pl.BlockSpec(memory_space=space(i)) for i in range(len(args))],
         out_specs=[pl.BlockSpec(memory_space=pltpu.VMEM) for _ in outs],
-        scratch_shapes=[pltpu.VMEM(s, F32) for s in scratch],
+        scratch_shapes=[pltpu.VMEM(s, F32) if isinstance(s, tuple) else s for s in scratch],
         compiler_params=pltpu.CompilerParams(vmem_limit_bytes=mib << 20),
+        cost_estimate=pl.CostEstimate(flops=int(cost), bytes_accessed=1 << 20, transcendentals=0),
         name=name,
     )(*args)
 
@@ -280,27 +308,34 @@
     band = FP // rows
     holes = dark_hole.shape[0]
     groups = estimate.shape[1] // LANES
-    share, mask = call(
-        pick_kernel, "pick", [(cols, 1, tile_rows), (band, FP)],
-        [estimate, dark_hole.reshape(1, holes)],
-        scratch=[(groups, LANES), (band * FP // LANES, LANES)],
+    dark_hole = dark_hole.reshape(1, holes)
+    (share,) = call(
+        pick_kernel, "pick", [(cols, 1, tile_rows)], [estimate, dark_hole], hbm=(0, 1),
+        scratch=[
+            estimate.shape, pltpu.VMEM((1, holes), jnp.int32), (groups, LANES),
+            pltpu.SemaphoreType.DMA, pltpu.SemaphoreType.DMA,
+        ],
     )
     share = exchange(share, "cols")
-    (grad,) = call(gradient_kernel, "gradient", [(rows, 1, width)], [share, jacobian], mib=14)
+    table = jax.ShapeDtypeStruct((waves, FP, 2 * PUP), BF16)
+    table_hi, table_lo = call(table_kernel, "tables", [table, table], [wavelengths], smem=(0,))
+    (grad,) = call(gradient_kernel, "gradient", [(rows, 1, width)], [share, jacobian])
     grad = exchange(grad, "rows")
-    (modal,) = call(modal_kernel, "modal", [(cols, 1, modes)], [grad, basis], mib=14)
+    (mask,) = call(mask_kernel, "mask", [(band, FP)], [dark_hole], scratch=[(band * FP // LANES, LANES)])
+    (modal,) = call(modal_kernel, "modal", [(cols, 1, modes)], [grad, basis])
     modal = exchange(modal, "cols")
     (parts,) = call(
         command_kernel, "commands", [(rows, cands, width)],
-        [modal, eigenvalues.reshape(1, modes), exponents, basis], smem=(2,), mib=20,
+        [modal, eigenvalues.reshape(1, modes), exponents, basis], smem=(2,),
     )
     parts = exchange(parts, "rows")
-    commands, chosen = call(gather_kernel, "gather", [(cands, width), (cols, 1, width)], [parts])
+    (chosen,) = call(send_kernel, "send", [(cols, 1, width)], [parts])
     chosen = exchange(chosen, "cols")
+    (commands,) = call(total_kernel, "total", [(cands, width)], [parts])
     intensity, stat = call(
         check_kernel, "check", [(waves, band, FP), (rows, 1, LANES)],
-        [chosen, influence, aberration, amplitude, wavelengths, mask],
-        scratch=[(2 * ACT, LANES), (PUP, PUP), (FP, 2 * PUP), (FP, 2 * PUP)], smem=(4,), mib=24,
+        [chosen, influence, aberration, amplitude, wavelengths, mask, table_hi, table_lo],
+        scratch=[(2 * ACT, LANES), (PUP, PUP)], smem=(4,),
     )
     stat = exchange(stat, "rows")
     image, contrast = call(

time: 95.9 us -> 93.1 us (0.971)
  blocking collectives: 46.4 us -> 26.4 us
  starting transfers between devices: 7.02 us -> 17.6 us
  waiting for transfers between devices: 13.2 us -> 18.1 us
  Pallas kernels: 14.4 us -> 17.4 us
  local copies, waits for them, and re-layouts: 13.5 us -> 12.1 us
    all_to_all x4 -> x2, blocking collectives: 46.4 us -> 26.4 us  [exchange(): return lax.all_to_all(x, axis, 0, 0)]
    all_to_all x2 -> x4, starting transfers between devices: 7.02 us -> 17.6 us  [exchange(): return lax.all_to_all(x, axis, 0, 0)]
    all_to_all x2 -> x4, waiting for transfers between devices: 13.2 us -> 18.1 us  [exchange(): return lax.all_to_all(x, axis, 0, 0)]
    pallas_call x7 -> x10, Pallas kernels: 14.4 us -> 17.4 us  [call(): pl.pallas_call(kernel, out_shape=[s if isinstance(s, jax.ShapeDtypeStruct...]
    unnamed x23 -> x39, local copies, waits for them, and re-layouts: 13.5 us -> 12.1 us
  transfers between devices with their start and end apart: 2 -> 4, of which waited for: 2 -> 4; matrix products, arithmetic and copies ran while one was open for 0% -> 1% of each run, Pallas kernels for 0% -> 4%
where the time goes in v2:
time: 93.1 us; the launch traced here: 92.5 us
  blocking collectives  26.4 us (28%)
  waiting for transfers between devices  18.1 us (19%)
  starting transfers between devices  17.6 us (19%)
  Pallas kernels  17.4 us (19%)
  local copies, waits for them, and re-layouts  12.1 us (13%)
    all_to_all x2, blocking collectives, exchange(): return lax.all_to_all(x, axis, 0, 0)  26.4 us
    all_to_all x4, waiting for transfers between devices, exchange(): return lax.all_to_all(x, axis, 0, 0)  18.1 us
    all_to_all x4, starting transfers between devices, exchange(): return lax.all_to_all(x, axis, 0, 0)  17.6 us
    pallas_call x10, Pallas kernels, call(): pl.pallas_call(kernel, out_shape=[s if isinstance(s, jax.ShapeDtypeStruct...  17.4 us
    unnamed x39, local copies, waits for them, and re-layouts  12.1 us
  transfers between devices with their start and end apart: 4, of which 4 were waited for; matrix products, arithmetic and copies ran while one was open for 1% of the time, Pallas kernels for 4%

profile of v2, /device:TPU:1, one launch (start us, length us, event | category | flops | bytes accessed | tf_op | source)
XLA Modules:
  0.0 92.5 jit_solution(16569052227848934601)
XLA Ops:
  0.6 0.9 copy-done.4
  1.5 0.7 copy-done.5
  2.3 1.1 %pick.1 = f32[16,1,2048]{2,1,0:T(1,128)S(1)} custom-call(f32[4,9216]{1,0:T(4,128)S(1)} %copy-done.4, s32[1,4096]{1,0:T(1,128)S(1)} %bitcast.3), custom_call_target="tpu_custom_call" | custom-call | flops 20000000000 | bytes 1048576 | tf_op jit(solution)/shard_map/pick/pallas_call | solution.py:285
  3.4 14.5 %all_to_all.30.field_ref = f32[16,1,2048]{2,1,0:T(1,128)S(1)} all-to-all(f32[16,1,2048]{2,1,0:T(1,128)S(1)} %pick.1), channel_id=1, replica_groups=mesh['rows'=8,'cols'=16] {'cols'}, dimensions={0} | all-to-all | bytes 262144 | tf_op jit(solution)/shard_map/all_to_all | solution.py:298
  17.9 0.7 gradient.1
  18.7 11.9 %all_to_all.31.grad_ref = f32[8,1,1152]{2,1,0:T(1,128)S(1)} all-to-all(f32[8,1,1152]{2,1,0:T(1,128)S(1)} %gradient.1), channel_id=1, replica_groups=mesh['rows'=8,'cols'=16] {'rows'}, dimensions={0} | all-to-all | bytes 73728 | tf_op jit(solution)/shard_map/all_to_all | solution.py:298
  30.6 0.0 copy-start.15
  30.6 0.0 copy-start.7
  30.6 1.4 %modal.1 = f32[16,1,2304]{2,1,0:T(1,128)} custom-call(f32[8,1,1152]{2,1,0:T(1,128)S(1)} %all_to_all.31.grad_ref, f32[2304,1152]{1,0:T(8,128)S(1)} %bitcast.2), custom_call_target="tpu_custom_call" | custom-call | flops 20000000000 | bytes 1048576 | tf_op jit(solution)/shard_map/modal/pallas_call | solution.py:285
  32.1 3.5 %all-to-all-start.2 = ((f32[16,1,2304]{2,1,0:T(1,128)}), f32[16,1,2304]{2,1,0:T(1,128)S(1)}, u32[]{:S(2)}, u32[]{:S(2)}) async-start(f32[16,1,2304]{2,1,0:T(1,128)} %modal.1), calls=%async_computation.2 | async-start | bytes 294912 | tf_op jit(solution)/shard_map/all_to_all | solution.py:298
  35.6 6.9 %all-to-all-done.2.modal_ref = f32[16,1,2304]{2,1,0:T(1,128)S(1)} async-done(((f32[16,1,2304]{2,1,0:T(1,128)}), f32[16,1,2304]{2,1,0:T(1,128)S(1)}, u32[]{:S(2)}, u32[]{:S(2)}) %all-to-all-start.2) | async-done | bytes 147488 | tf_op jit(solution)/shard_map/all_to_all | solution.py:298
  42.5 4.0 %copy-done = f32[2304,1152]{1,0:T(8,128)S(1)} copy-done((f32[2304,1152]{1,0:T(8,128)S(1)}, f32[2304,1152]{1,0:T(8,128)}, u32[]{:S(2)}) %copy-start) | copy-done | bytes 10616856
  46.5 3.0 %commands.1 = f32[8,8,1152]{2,1,0:T(8,128)} custom-call(f32[16,1,2304]{2,1,0:T(1,128)S(1)} %all-to-all-done.2.modal_ref, f32[1,2304]{1,0:T(1,128)S(1)} %reshape.13.eig_ref, s32[8]{0:T(128)S(1)} %copy-done.7, f32[2304,1152]{1,0:T(8,128)S(1)} %copy-done), custom_call_target="tpu_custom_call" | custom-call | flops 20000000000 | bytes 1048576 | tf_op jit(solution)/shard_map/commands/pallas_call | solution.py:285
  49.5 5.2 %all-to-all-start.3 = ((f32[8,8,1152]{2,1,0:T(8,128)}), f32[8,8,1152]{2,1,0:T(8,128)S(1)}, u32[]{:S(2)}, u32[]{:S(2)}) async-start(f32[8,8,1152]{2,1,0:T(8,128)} %commands.1), calls=%async_computation.3 | async-start | bytes 589824 | tf_op jit(solution)/shard_map/all_to_all | solution.py:298
  54.7 0.5 mask.1.mask_ref
  55.2 0.6 copy-done.13
  55.8 5.7 %all-to-all-done.3.parts_ref = f32[8,8,1152]{2,1,0:T(8,128)S(1)} async-done(((f32[8,8,1152]{2,1,0:T(8,128)}), f32[8,8,1152]{2,1,0:T(8,128)S(1)}, u32[]{:S(2)}, u32[]{:S(2)}) %all-to-all-start.3) | async-done | bytes 294944 | tf_op jit(solution)/shard_map/all_to_all | solution.py:298
  61.5 0.7 send.1
  62.2 3.5 %all-to-all-start.4 = ((f32[16,1,1152]{2,1,0:T(1,128)}), f32[16,1,1152]{2,1,0:T(1,128)S(1)}, u32[]{:S(2)}, u32[]{:S(2)}) async-start(f32[16,1,1152]{2,1,0:T(1,128)} %send.1), calls=%async_computation.4 | async-start | bytes 147456 | tf_op jit(solution)/shard_map/all_to_all | solution.py:298
  65.7 0.0 copy-start.2
  65.7 2.4 %tables.1 = (bf16[6,384,512]{2,1,0:T(8,128)(2,1)S(1)}, bf16[6,384,512]{2,1,0:T(8,128)(2,1)S(1)}) custom-call(f32[12]{0:T(128)S(1)} %copy-done.8), custom_call_target="tpu_custom_call" | custom-call | flops 20000000000 | bytes 1048576 | tf_op jit(solution)/shard_map/tables/pallas_call | solution.py:285
  68.1 1.4 %copy-done.9 = bf16[6,384,512]{2,1,0:T(8,128)(2,1)} copy-done((bf16[6,384,512]{2,1,0:T(8,128)(2,1)}, bf16[6,384,512]{2,1,0:T(8,128)(2,1)S(1)}, u32[]{:S(2)}) %copy-start.9) | copy-done | bytes 2359320
  69.5 1.0 %copy.13.infl_ref = f32[2,256,96]{2,1,0:T(8,128)S(1)} copy(f32[2,256,96]{1,2,0:T(8,128)} %param.19) | data formatting | bytes 393216 | tf_op args[9]
  70.6 1.6 %all-to-all-done.4.cmd_ref = f32[16,1,1152]{2,1,0:T(1,128)S(1)} async-done(((f32[16,1,1152]{2,1,0:T(1,128)}), f32[16,1,1152]{2,1,0:T(1,128)S(1)}, u32[]{:S(2)}, u32[]{:S(2)}) %all-to-all-start.4) | async-done | bytes 73760 | tf_op jit(solution)/shard_map/all_to_all | solution.py:298
  72.2 1.7 %copy-done.10 = bf16[6,384,512]{2,1,0:T(8,128)(2,1)S(1)} copy-done((bf16[6,384,512]{2,1,0:T(8,128)(2,1)S(1)}, bf16[6,384,512]{2,1,0:T(8,128)(2,1)}, u32[]{:S(2)}) %copy-start.10) | copy-done | bytes 2359320
  73.9 0.9 copy-done.14
  74.7 6.1 %check.1 = (f32[6,48,384]{2,1,0:T(8,128)S(1)}, f32[8,1,128]{2,1,0:T(1,128)}) custom-call(f32[16,1,1152]{2,1,0:T(1,128)S(1)} %all-to-all-done.4.cmd_ref, f32[2,256,96]{2,1,0:T(8,128)S(1)} %copy.13.infl_ref, f32[256,256]{1,0:T(8,128)S(1)} %copy-done.2, f32[256,256]{1,0:T(8,128)S(1)} %copy-done.3, f32[12]{0:T(128)S(1)} %copy-done.8, f32[48,384]{1,0:T(8,128)S(1)} %copy-done.14, ...), custom_call_target="tpu_custom_call" | custom-call | flops 20000000000 | bytes 1048576 | tf_op jit(solution)/shard_map/check/pallas_call | solution.py:285
  80.8 0.8 copy-done.11
  81.6 5.4 %all-to-all-start.5 = ((f32[8,1,128]{2,1,0:T(1,128)}), f32[8,1,128]{2,1,0:T(1,128)S(1)}, u32[]{:S(2)}, u32[]{:S(2)}) async-start(f32[8,1,128]{2,1,0:T(1,128)} %get-tuple-element.11), calls=%async_computation.5 | async-start | bytes 8192 | tf_op jit(solution)/shard_map/all_to_all | solution.py:298
  87.0 0.6 total.1
  87.6 4.0 %all-to-all-done.5.stat_ref = f32[8,1,128]{2,1,0:T(1,128)S(1)} async-done(((f32[8,1,128]{2,1,0:T(1,128)}), f32[8,1,128]{2,1,0:T(1,128)S(1)}, u32[]{:S(2)}, u32[]{:S(2)}) %all-to-all-start.5) | async-done | bytes 4128 | tf_op jit(solution)/shard_map/all_to_all | solution.py:298
  91.6 0.9 scale.1
  (29 shorter events, 0.1 us)
Async XLA Ops:
  0.6 0.9 copy-start.4
  1.5 0.7 copy-start.5
  2.3 15.7 %copy-start.1 = (f32[2048,1152]{1,0:T(8,128)S(1)}, f32[2048,1152]{1,0:T(8,128)}, u32[]{:S(2)}) copy-start(f32[2048,1152]{1,0:T(8,128)} %jac_ref.1) | copy-start | bytes 28311556
  2.3 28.3 %slice-start = ((s8[10616832]{0:T(1024)(128)(4,1)}), s8[4194304]{0:T(1024)(128)(4,1)S(1)}, s32[]{:S(2)}) async-start(s8[10616832]{0:T(1024)(128)(4,1)} %bitcast.1), calls=%async_computation.6 | async-start | bytes 8388608
  2.3 28.3 %slice-start.1 = ((s8[10616832]{0:T(1024)(128)(4,1)}), s8[4194304]{0:T(1024)(128)(4,1)S(1)}, s32[]{:S(2)}) async-start(s8[10616832]{0:T(1024)(128)(4,1)} %bitcast.1), calls=%async_computation.7 | async-start | bytes 8388608
  17.9 12.7 %slice-start.2 = ((s8[10616832]{0:T(1024)(128)(4,1)}), s8[2228224]{0:T(1024)(128)(4,1)S(1)}, s32[]{:S(2)}) async-start(s8[10616832]{0:T(1024)(128)(4,1)} %bitcast.1), calls=%async_computation.8 | async-start | bytes 4456448
  30.6 5.0 %copy-start.15 = (f32[2304]{0:T(1024)S(1)}, f32[2304]{0:T(1024)}, u32[]{:S(2)}) copy-start(f32[2304]{0:T(1024)} %param.14) | copy-start | bytes 27652
  30.6 11.9 %copy-start.7 = (s32[8]{0:T(128)S(1)}, s32[8]{0:T(128)}, u32[]{:S(2)}) copy-start(s32[8]{0:T(128)} %exp_ref.1) | copy-start | bytes 100
  32.1 10.4 %all-to-all-start.2 = ((f32[16,1,2304]{2,1,0:T(1,128)}), f32[16,1,2304]{2,1,0:T(1,128)S(1)}, u32[]{:S(2)}, u32[]{:S(2)}) async-start(f32[16,1,2304]{2,1,0:T(1,128)} %modal.1), calls=%async_computation.2 | async-start | bytes 294912 | tf_op jit(solution)/shard_map/all_to_all | solution.py:298
  42.5 4.0 %copy-start = (f32[2304,1152]{1,0:T(8,128)S(1)}, f32[2304,1152]{1,0:T(8,128)}, u32[]{:S(2)}) copy-start(f32[2304,1152]{1,0:T(8,128)} %basis_ref.3) | copy-start | bytes 31850500
  46.5 8.2 %copy-start.6 = (s32[4096]{0:T(1024)S(1)}, s32[4096]{0:T(1024)}, u32[]{:S(2)}) copy-start(s32[4096]{0:T(1024)} %param.11) | copy-start | bytes 49156
  49.5 12.0 %all-to-all-start.3 = ((f32[8,8,1152]{2,1,0:T(8,128)}), f32[8,8,1152]{2,1,0:T(8,128)S(1)}, u32[]{:S(2)}, u32[]{:S(2)}) async-start(f32[8,8,1152]{2,1,0:T(8,128)} %commands.1), calls=%async_computation.3 | async-start | bytes 589824 | tf_op jit(solution)/shard_map/all_to_all | solution.py:298
  55.2 0.6 copy-start.13
  55.8 9.9 %copy-start.8 = (f32[12]{0:T(128)S(1)}, f32[12]{0:T(128)}, u32[]{:S(2)}) copy-start(f32[12]{0:T(128)} %wave_ref.3) | copy-start | bytes 148
  62.2 10.0 %all-to-all-start.4 = ((f32[16,1,1152]{2,1,0:T(1,128)}), f32[16,1,1152]{2,1,0:T(1,128)S(1)}, u32[]{:S(2)}, u32[]{:S(2)}) async-start(f32[16,1,1152]{2,1,0:T(1,128)} %send.1), calls=%async_computation.4 | async-start | bytes 147456 | tf_op jit(solution)/shard_map/all_to_all | solution.py:298
  65.7 6.5 %copy-start.2 = (f32[256,256]{1,0:T(8,128)S(1)}, f32[256,256]{1,0:T(8,128)}, u32[]{:S(2)}) copy-start(f32[256,256]{1,0:T(8,128)} %aber_ref.1) | copy-start | bytes 786436
  65.7 6.5 %copy-start.3 = (f32[256,256]{1,0:T(8,128)S(1)}, f32[256,256]{1,0:T(8,128)}, u32[]{:S(2)}) copy-start(f32[256,256]{1,0:T(8,128)} %amp_ref.1) | copy-start | bytes 786436
  68.1 1.4 %copy-start.9 = (bf16[6,384,512]{2,1,0:T(8,128)(2,1)}, bf16[6,384,512]{2,1,0:T(8,128)(2,1)S(1)}, u32[]{:S(2)}) copy-start(bf16[6,384,512]{2,1,0:T(8,128)(2,1)S(1)} %get-tuple-element.10.lo_ref) | copy-start | bytes 7077892
  72.2 1.7 %copy-start.10 = (bf16[6,384,512]{2,1,0:T(8,128)(2,1)S(1)}, bf16[6,384,512]{2,1,0:T(8,128)(2,1)}, u32[]{:S(2)}) copy-start(bf16[6,384,512]{2,1,0:T(8,128)(2,1)} %copy-done.9) | copy-start | bytes 7077892
  73.9 0.9 copy-start.14
  80.8 0.8 copy-start.11
  81.6 10.0 %all-to-all-start.5 = ((f32[8,1,128]{2,1,0:T(1,128)}), f32[8,1,128]{2,1,0:T(1,128)S(1)}, u32[]{:S(2)}, u32[]{:S(2)}) async-start(f32[8,1,128]{2,1,0:T(1,128)} %get-tuple-element.11), calls=%async_computation.5 | async-start | bytes 8192 | tf_op jit(solution)/shard_map/all_to_all | solution.py:298
  87.0 4.6 %copy-start.12 = (f32[6,48,384]{2,1,0:T(8,128)S(1)}, f32[6,48,384]{2,1,0:T(8,128)}, u32[]{:S(2)}) copy-start(f32[6,48,384]{2,1,0:T(8,128)} %copy-done.11) | copy-start | bytes 1327108

commit v3 on v1

--- a/solution.py
+++ b/solution.py
@@ -48,8 +48,8 @@
     return lax.dot_general(a, b, (((1,), (1,)), ((), ())), preferred_element_type=F32, precision=precision)
 
 
-def tdot(a, b):
-    return lax.dot_general(a, b, (((0,), (0,)), ((), ())), preferred_element_type=F32)
+def tdot(a, b, precision=None):
+    return lax.dot_general(a, b, (((0,), (0,)), ((), ())), preferred_element_type=F32, precision=precision)
 
 
 def spread(ref, row):
@@ -139,6 +139,7 @@
 
 def command_kernel(modal_ref, eig_ref, exp_ref, basis_ref, out_ref):
     modal = gathered_sum(modal_ref)
+    eigen = eig_ref[...].reshape(modal.shape)
     cands = exp_ref.shape[0]
     tile_rows, width = basis_ref.shape
     step = 256
@@ -150,7 +151,7 @@
     acc = jnp.zeros((2 * cands, width), F32)
     for b in range(tile_rows // step):
         at = slice(b * step, (b + 1) * step)
-        weights = -modal[:, at] / (eig_ref[:, at] + damping)
+        weights = -modal[:, at] / (eigen[:, at] + damping)
         high = weights.astype(BF16).astype(F32)
         both = jnp.concatenate([high, weights - high], axis=0).astype(BF16)
         hi, lo = split2(basis_ref[at, :])
@@ -176,7 +177,7 @@
     waves, band, full = out_ref.shape
     pup = aber_ref.shape[0]
     blocks = cmd_ref.shape[0]
-    acts = infl_ref.shape[2]
+    acts = infl_ref.shape[1]
     mirrors = infl_ref.shape[0]
     groups_count = wave_ref.shape[0] // waves
     first_wave = (col % groups_count) * waves
@@ -188,8 +189,9 @@
         for a in range(per_block):
             act_ref[pl.ds(m * acts + a, per_mirror, stride=per_block), :acts] = part[:, a * acts : (a + 1) * acts]
         actuators = act_ref[m * acts : (m + 1) * acts, :acts]
-        right = mm_t(actuators, infl_ref[m], HIGHEST)
-        surface = surface + jnp.dot(infl_ref[m], right, precision=HIGHEST, preferred_element_type=F32)
+        influence = infl_ref[m]
+        right = jnp.dot(actuators, influence, precision=HIGHEST, preferred_element_type=F32)
+        surface = surface + tdot(influence, right, HIGHEST)
     height_ref[...] = aber_ref[...] + (2.0 * STROKE) * surface
     place = (lax.broadcasted_iota(jnp.int32, (1, pup), 1).astype(F32) - (pup / 2 - 0.5)) * (1.0 / pup)
     near = lax.broadcasted_iota(jnp.int32, (8, 1), 0).astype(F32) - (full / 2 - 0.5)
@@ -253,15 +255,15 @@
         out_ref[w] = int_ref[w] * inverse[:, w : w + 1]
 
 
-def call(kernel, name, outs, args, scratch=(), smem=(), mib=8):
-    specs = [pl.BlockSpec(memory_space=pltpu.SMEM if i in smem else pltpu.VMEM) for i in range(len(args))]
+def call(kernel, name, outs, args, scratch=(), smem=()):
     return pl.pallas_call(
         kernel,
         out_shape=[jax.ShapeDtypeStruct(s, F32) for s in outs],
-        in_specs=specs,
+        in_specs=[pl.BlockSpec(memory_space=pltpu.SMEM if i in smem else pltpu.VMEM) for i in range(len(args))],
         out_specs=[pl.BlockSpec(memory_space=pltpu.VMEM) for _ in outs],
         scratch_shapes=[pltpu.VMEM(s, F32) for s in scratch],
-        compiler_params=pltpu.CompilerParams(vmem_limit_bytes=mib << 20),
+        compiler_params=pltpu.CompilerParams(vmem_limit_bytes=16 << 20),
+        cost_estimate=pl.CostEstimate(flops=20_000_000_000, bytes_accessed=1 << 20, transcendentals=0),
         name=name,
     )(*args)
 
@@ -286,21 +288,21 @@
         scratch=[(groups, LANES), (band * FP // LANES, LANES)],
     )
     share = exchange(share, "cols")
-    (grad,) = call(gradient_kernel, "gradient", [(rows, 1, width)], [share, jacobian], mib=14)
+    (grad,) = call(gradient_kernel, "gradient", [(rows, 1, width)], [share, jacobian])
     grad = exchange(grad, "rows")
-    (modal,) = call(modal_kernel, "modal", [(cols, 1, modes)], [grad, basis], mib=14)
+    (modal,) = call(modal_kernel, "modal", [(cols, 1, modes)], [grad, basis])
     modal = exchange(modal, "cols")
     (parts,) = call(
         command_kernel, "commands", [(rows, cands, width)],
-        [modal, eigenvalues.reshape(1, modes), exponents, basis], smem=(2,), mib=20,
+        [modal, eigenvalues, exponents, basis], smem=(2,),
     )
     parts = exchange(parts, "rows")
     commands, chosen = call(gather_kernel, "gather", [(cands, width), (cols, 1, width)], [parts])
     chosen = exchange(chosen, "cols")
     intensity, stat = call(
         check_kernel, "check", [(waves, band, FP), (rows, 1, LANES)],
-        [chosen, influence, aberration, amplitude, wavelengths, mask],
-        scratch=[(2 * ACT, LANES), (PUP, PUP), (FP, 2 * PUP), (FP, 2 * PUP)], smem=(4,), mib=24,
+        [chosen, jnp.swapaxes(influence, 1, 2), aberration, amplitude, wavelengths, mask],
+        scratch=[(2 * ACT, LANES), (PUP, PUP), (FP, 2 * PUP), (FP, 2 * PUP)], smem=(4,),
     )
     stat = exchange(stat, "rows")
     image, contrast = call(

time: 95.9 us -> 82.7 us (0.86)
  blocking collectives: 46.4 us -> 66.2 us
  waiting for transfers between devices: 13.2 us -> 0 us
  local copies, waits for them, and re-layouts: 13.5 us -> 1.66 us
  starting transfers between devices: 7.02 us -> 0 us
    all_to_all x4 -> x6, blocking collectives: 46.4 us -> 66.2 us  [exchange(): return lax.all_to_all(x, axis, 0, 0)]
    all_to_all x2 -> x0, waiting for transfers between devices: 13.2 us -> none  [exchange(): return lax.all_to_all(x, axis, 0, 0)]
    unnamed x23 -> x24, local copies, waits for them, and re-layouts: 13.5 us -> 1.66 us
    all_to_all x2 -> x0, starting transfers between devices: 7.02 us -> none  [exchange(): return lax.all_to_all(x, axis, 0, 0)]
  transfers between devices with their start and end apart: 2 -> 0, of which waited for: 2 -> 0; matrix products, arithmetic and copies ran while one was open for 0% -> 0% of each run, Pallas kernels for 0% -> 0%
where the time goes in v3:
time: 82.7 us; the launch traced here: 82.3 us
  blocking collectives  66.2 us (80%)
  Pallas kernels  13.7 us (17%)
  local copies, waits for them, and re-layouts  1.66 us (2%)
    all_to_all x6, blocking collectives, exchange(): return lax.all_to_all(x, axis, 0, 0)  66.2 us
    pallas_call x7, Pallas kernels, call(): pl.pallas_call(kernel, out_shape=[jax.ShapeDtypeStruct(s, F32) for s in o...  13.7 us
    unnamed x24, local copies, waits for them, and re-layouts  1.66 us

profile of v3, /device:TPU:1, one launch (start us, length us, event | category | flops | bytes accessed | tf_op | source)
XLA Modules:
  0.0 82.3 jit_solution(13571017329087359463)
XLA Ops:
  0.6 0.0 copy-start.4
  0.6 0.9 %copy-done.4 = f32[4,9216]{1,0:T(4,128)S(1)} copy-done((f32[4,9216]{1,0:T(4,128)S(1)}, f32[4,9216]{1,0:T(4,128)}, u32[]{:S(2)}) %copy-start.4) | copy-done | bytes 147480
  1.5 0.0 copy-start.5
  1.5 0.7 copy-done.5
  2.3 0.0 copy-start
  2.3 0.0 slice-start
  2.3 0.0 slice-start.1
  2.3 1.4 %pick.1 = (f32[16,1,2048]{2,1,0:T(1,128)S(1)}, f32[48,384]{1,0:T(8,128)S(1)}) custom-call(f32[4,9216]{1,0:T(4,128)S(1)} %copy-done.4, s32[1,4096]{1,0:T(1,128)S(1)} %bitcast.5), custom_call_target="tpu_custom_call" | custom-call | flops 20000000000 | bytes 1048576 | tf_op jit(solution)/shard_map/pick/pallas_call | solution.py:259
  3.7 14.5 %all_to_all.30.field_ref = f32[16,1,2048]{2,1,0:T(1,128)S(1)} all-to-all(f32[16,1,2048]{2,1,0:T(1,128)S(1)} %get-tuple-element.11), channel_id=1, replica_groups=mesh['rows'=8,'cols'=16] {'cols'}, dimensions={0} | all-to-all | bytes 262144 | tf_op jit(solution)/shard_map/all_to_all | solution.py:272
  18.2 0.0 copy-done
  18.2 0.7 gradient.1
  18.9 11.9 %all_to_all.31.grad_ref = f32[8,1,1152]{2,1,0:T(1,128)S(1)} all-to-all(f32[8,1,1152]{2,1,0:T(1,128)S(1)} %gradient.1), channel_id=1, replica_groups=mesh['rows'=8,'cols'=16] {'rows'}, dimensions={0} | all-to-all | bytes 73728 | tf_op jit(solution)/shard_map/all_to_all | solution.py:272
  30.8 0.0 slice-done
  30.8 0.0 slice-done.1
  30.9 0.0 slice-done.2
  30.9 0.0 copy-start.6
  30.9 0.0 copy-start.7
  30.9 0.8 modal.1
  31.7 9.8 %all_to_all.32.modal_ref = f32[16,1,2304]{2,1,0:T(1,128)S(1)} all-to-all(f32[16,1,2304]{2,1,0:T(1,128)S(1)} %modal.1), channel_id=1, replica_groups=mesh['rows'=8,'cols'=16] {'cols'}, dimensions={0} | all-to-all | bytes 294912 | tf_op jit(solution)/shard_map/all_to_all | solution.py:272
  41.5 0.0 copy-done.6
  41.5 0.0 copy-done.7
  41.5 2.2 %commands.1 = f32[8,8,1152]{2,1,0:T(8,128)S(1)} custom-call(f32[16,1,2304]{2,1,0:T(1,128)S(1)} %all_to_all.32.modal_ref, f32[2304]{0:T(1024)S(1)} %copy-done.6, s32[8]{0:T(128)S(1)} %copy-done.7, f32[2304,1152]{1,0:T(8,128)S(1)} %bitcast.3), custom_call_target="tpu_custom_call" | custom-call | flops 20000000000 | bytes 1048576 | tf_op jit(solution)/shard_map/commands/pallas_call | solution.py:259
  43.7 11.8 %all_to_all.33.parts_ref = f32[8,8,1152]{2,1,0:T(8,128)S(1)} all-to-all(f32[8,8,1152]{2,1,0:T(8,128)S(1)} %commands.1), channel_id=1, replica_groups=mesh['rows'=8,'cols'=16] {'rows'}, dimensions={0} | all-to-all | bytes 589824 | tf_op jit(solution)/shard_map/all_to_all | solution.py:272
  55.5 0.6 gather.1
  56.1 9.3 %all_to_all.34.cmd_ref = f32[16,1,1152]{2,1,0:T(1,128)S(1)} all-to-all(f32[16,1,1152]{2,1,0:T(1,128)S(1)} %get-tuple-element.13), channel_id=1, replica_groups=mesh['rows'=8,'cols'=16] {'cols'}, dimensions={0} | all-to-all | bytes 147456 | tf_op jit(solution)/shard_map/all_to_all | solution.py:272
  65.5 0.0 copy-done.1
  65.5 0.0 copy-done.2
  65.5 0.0 copy-done.3
  65.5 0.0 copy-done.8
  65.5 7.0 %check.1 = (f32[6,48,384]{2,1,0:T(8,128)S(1)}, f32[8,1,128]{2,1,0:T(1,128)S(1)}) custom-call(f32[16,1,1152]{2,1,0:T(1,128)S(1)} %all_to_all.34.cmd_ref, f32[2,96,256]{2,1,0:T(8,128)S(1)} %bitcast.4, f32[256,256]{1,0:T(8,128)S(1)} %copy-done.1, f32[256,256]{1,0:T(8,128)S(1)} %copy-done.2, f32[12]{0:T(128)S(1)} %copy-done.8, ...), custom_call_target="tpu_custom_call" | custom-call | flops 20000000000 | bytes 1048576 | tf_op jit(solution)/shard_map/check/pallas_call | solution.py:259
  72.5 8.9 %all_to_all.35.stat_ref = f32[8,1,128]{2,1,0:T(1,128)S(1)} all-to-all(f32[8,1,128]{2,1,0:T(1,128)S(1)} %get-tuple-element.15), channel_id=1, replica_groups=mesh['rows'=8,'cols'=16] {'rows'}, dimensions={0} | all-to-all | bytes 8192 | tf_op jit(solution)/shard_map/all_to_all | solution.py:272
  81.4 0.9 %scale.1 = (f32[6,48,384]{2,1,0:T(8,128)}, f32[1,6]{1,0:T(1,128)}) custom-call(f32[8,1,128]{2,1,0:T(1,128)S(1)} %all_to_all.35.stat_ref, f32[6,48,384]{2,1,0:T(8,128)S(1)} %get-tuple-element.16.int_ref), custom_call_target="tpu_custom_call" | custom-call | flops 20000000000 | bytes 1048576 | tf_op jit(solution)/shard_map/scale/pallas_call | solution.py:259
  (6 shorter events, 0.0 us)
Async XLA Ops:
  0.6 0.9 %copy-start.4 = (f32[4,9216]{1,0:T(4,128)S(1)}, f32[4,9216]{1,0:T(4,128)}, u32[]{:S(2)}) copy-start(f32[4,9216]{1,0:T(4,128)} %est_ref.1) | copy-start | bytes 442372
  1.5 0.7 copy-start.5
  2.3 15.9 %copy-start = (f32[2048,1152]{1,0:T(8,128)S(1)}, f32[2048,1152]{1,0:T(8,128)}, u32[]{:S(2)}) copy-start(f32[2048,1152]{1,0:T(8,128)} %jac_ref.1) | copy-start | bytes 28311556
  2.3 28.6 %slice-start = ((s8[10616832]{0:T(1024)(128)(4,1)}), s8[4194304]{0:T(1024)(128)(4,1)S(1)}, s32[]{:S(2)}) async-start(s8[10616832]{0:T(1024)(128)(4,1)} %bitcast.2), calls=%async_computation.6 | async-start | bytes 8388608
  2.3 28.6 %slice-start.1 = ((s8[10616832]{0:T(1024)(128)(4,1)}), s8[4194304]{0:T(1024)(128)(4,1)S(1)}, s32[]{:S(2)}) async-start(s8[10616832]{0:T(1024)(128)(4,1)} %bitcast.2), calls=%async_computation.7 | async-start | bytes 8388608
  18.2 12.7 %slice-start.2 = ((s8[10616832]{0:T(1024)(128)(4,1)}), s8[2228224]{0:T(1024)(128)(4,1)S(1)}, s32[]{:S(2)}) async-start(s8[10616832]{0:T(1024)(128)(4,1)} %bitcast.2), calls=%async_computation.8 | async-start | bytes 4456448
  30.9 10.6 %copy-start.6 = (f32[2304]{0:T(1024)S(1)}, f32[2304]{0:T(1024)}, u32[]{:S(2)}) copy-start(f32[2304]{0:T(1024)} %eig_ref.1) | copy-start | bytes 27652
  30.9 10.6 %copy-start.7 = (s32[8]{0:T(128)S(1)}, s32[8]{0:T(128)}, u32[]{:S(2)}) copy-start(s32[8]{0:T(128)} %exp_ref.1) | copy-start | bytes 100
  55.5 10.0 %copy-start.1 = (f32[256,256]{1,0:T(8,128)S(1)}, f32[256,256]{1,0:T(8,128)}, u32[]{:S(2)}) copy-start(f32[256,256]{1,0:T(8,128)} %aber_ref.1) | copy-start | bytes 786436
  55.5 10.0 %copy-start.2 = (f32[256,256]{1,0:T(8,128)S(1)}, f32[256,256]{1,0:T(8,128)}, u32[]{:S(2)}) copy-start(f32[256,256]{1,0:T(8,128)} %amp_ref.1) | copy-start | bytes 786436
  55.5 10.0 %copy-start.3 = (f32[2,256,96]{1,2,0:T(8,128)S(1)}, f32[2,256,96]{1,2,0:T(8,128)}, u32[]{:S(2)}) copy-start(f32[2,256,96]{1,2,0:T(8,128)} %param.19) | copy-start | bytes 589828
  55.5 10.0 %copy-start.8 = (f32[12]{0:T(128)S(1)}, f32[12]{0:T(128)}, u32[]{:S(2)}) copy-start(f32[12]{0:T(128)} %wave_ref.1) | copy-start | bytes 148

commit v4 on v3

--- a/solution.py
+++ b/solution.py
@@ -16,10 +16,12 @@
 PIXEL_SCALE = 0.25
 F32 = jnp.float32
 BF16 = jnp.bfloat16
+LEAST = -2
+LEVELS = 6
 HIGHEST = lax.Precision.HIGHEST
 
-COS = (1.0, -19.73920440673828, 64.93911743164062, -85.45014190673828, 60.16762924194336, -25.967599868774414, 6.528658390045166)
-SIN = (6.2831854820251465, -41.34170150756836, 81.60513305664062, -76.70301818847656, 42.02592849731445, -14.899847030639648, 3.2381374835968018)
+COS = (0.9999992251396179, -19.738981246948242, 64.92865753173828, -85.27162170410156, 58.79049301147461, -21.07110595703125)
+SIN = (6.283185005187988, -41.341590881347656, 81.59994506835938, -76.61447143554688, 41.3428840637207, -12.471243858337402)
 
 
 def horner(coefs, x):
@@ -137,18 +139,14 @@
     spread(out_ref, jnp.concatenate(parts, axis=1))
 
 
-def command_kernel(modal_ref, eig_ref, exp_ref, basis_ref, out_ref):
+def command_kernel(modal_ref, eig_ref, basis_ref, out_ref):
     modal = gathered_sum(modal_ref)
     eigen = eig_ref[...].reshape(modal.shape)
-    cands = exp_ref.shape[0]
     tile_rows, width = basis_ref.shape
     step = 256
-    cand = lax.broadcasted_iota(jnp.int32, (cands, 1), 0)
-    power = jnp.zeros((cands, 1), F32)
-    for k in range(cands):
-        power = jnp.where(cand == k, exp_ref[k].astype(F32), power)
-    damping = jnp.exp2(power)
-    acc = jnp.zeros((2 * cands, width), F32)
+    rows = 8
+    damping = jnp.exp2((lax.broadcasted_iota(jnp.int32, (rows, 1), 0) + LEAST).astype(F32))
+    acc = jnp.zeros((2 * rows, width), F32)
     for b in range(tile_rows // step):
         at = slice(b * step, (b + 1) * step)
         weights = -modal[:, at] / (eigen[:, at] + damping)
@@ -156,93 +154,178 @@
         both = jnp.concatenate([high, weights - high], axis=0).astype(BF16)
         hi, lo = split2(basis_ref[at, :])
         acc = acc + mm(both, hi) + mm(both, lo)
-    commands = acc[:cands] + acc[cands:]
-    for j in range(out_ref.shape[0]):
-        out_ref[j] = commands
-
-
-def gather_kernel(parts_ref, out_ref, send_ref):
-    total = parts_ref[0]
-    for j in range(1, parts_ref.shape[0]):
-        total = total + parts_ref[j]
-    out_ref[...] = total
-    copies = send_ref.shape[0] // total.shape[0]
-    for j in range(send_ref.shape[0]):
-        send_ref[j] = total[j // copies : j // copies + 1]
-
-
-def check_kernel(cmd_ref, infl_ref, aber_ref, amp_ref, wave_ref, mask_ref, out_ref, stat_ref, act_ref, height_ref, hi_ref, lo_ref):
+    levels = acc[:rows] + acc[rows:]
+    spread(out_ref, jnp.concatenate([levels[l : l + 1] for l in range(LEVELS)], axis=1))
+
+
+def gather_kernel(parts_ref, exp_ref, out_ref, send_ref, levels_ref):
+    levels_ref[...] = gathered_sum(parts_ref)
+    cands, width = out_ref.shape
+    copies = send_ref.shape[0] // cands
+    for k in range(cands):
+        level = exp_ref[k] - LEAST
+        row = levels_ref[:, pl.ds(pl.multiple_of(level * width, LANES), width)]
+        out_ref[k : k + 1, :] = row
+        for j in range(copies):
+            send_ref[k * copies + j] = row
+
+
+def transform(near_u, far_u, turns):
+    near_c, near_s = cos_sin_turns(near_u * turns)
+    far_c, far_s = cos_sin_turns(far_u * turns)
+    cos = []
+    sin = []
+    for g in range(far_u.shape[0]):
+        fc = far_c[g : g + 1]
+        fs = far_s[g : g + 1]
+        cos.append(near_c * fc - near_s * fs)
+        sin.append(-(near_s * fc + near_c * fs))
+    return jnp.concatenate([jnp.concatenate(cos, axis=0), jnp.concatenate(sin, axis=0)], axis=1)
+
+
+def places(size, pup):
+    return (lax.broadcasted_iota(jnp.int32, (1, size), 1).astype(F32) - (pup / 2 - 0.5)) * (1.0 / pup)
+
+
+def mirror_surface(cmd_ref, infl_ref, half_refs):
+    blocks = cmd_ref.shape[0]
+    mirrors, acts, pup = infl_ref.shape
+    per_block = cmd_ref.shape[2] // acts
+    per_mirror = blocks // mirrors
+    lefts = []
+    for m in range(mirrors):
+        halves = []
+        for h in range(pup // LANES):
+            half_ref = half_refs[m * (pup // LANES) + h]
+            half_ref[...] = infl_ref[m, :, h * LANES : (h + 1) * LANES]
+            halves.append([half_ref[pl.ds(a, per_mirror, stride=per_block), :] for a in range(per_block)])
+        lefts.append(jnp.concatenate([jnp.concatenate(part, axis=0) for part in halves], axis=1))
+    left_hi, left_lo = split2(jnp.concatenate(lefts, axis=0).T)
+    rights = []
+    for m in range(mirrors):
+        part = jnp.concatenate([cmd_ref[m * per_mirror + j] for j in range(per_mirror)], axis=0)
+        act_hi, act_lo = split2(jnp.concatenate([part[:, a * acts : (a + 1) * acts] for a in range(per_block)], axis=0))
+        infl_hi, infl_lo = split2(infl_ref[m])
+        both = mm(jnp.concatenate([act_hi, act_lo], axis=0), infl_hi)
+        rights.append(both[:acts] + both[acts:] + mm(act_hi, infl_lo))
+    right_hi, right_lo = split2(jnp.concatenate(rights, axis=0))
+    both = mm(jnp.concatenate([left_hi, left_lo], axis=0), right_hi)
+    return both[:pup] + both[pup:] + mm(left_hi, right_lo)
+
+
+def turned(x):
+    half = x.shape[1] // 2
+    re = x[:, :half]
+    im = x[:, half:]
+    return jnp.concatenate([jnp.concatenate([re, -im], axis=1), jnp.concatenate([im, re], axis=1)], axis=0)
+
+
+def check_scratch(waves):
+    return [pltpu.SemaphoreType.DMA, pltpu.VMEM((PUP, PUP), F32)] + [pltpu.VMEM((ACT, LANES), F32)] * 4
+
+
+def check_kernel(cmd_ref, infl_ref, aber_ref, amp_ref, wave_ref, mask_ref, all_ref, out_ref, stat_ref, all_out, sem, height_ref, *half_refs):
+    whole = pltpu.make_async_copy(all_ref, all_out, sem)
+    whole.start()
     row = lax.axis_index("rows")
     col = lax.axis_index("cols")
     waves, band, full = out_ref.shape
     pup = aber_ref.shape[0]
-    blocks = cmd_ref.shape[0]
-    acts = infl_ref.shape[1]
-    mirrors = infl_ref.shape[0]
+    half = pup // 2
+    side = full // 2
     groups_count = wave_ref.shape[0] // waves
     first_wave = (col % groups_count) * waves
-    per_block = cmd_ref.shape[2] // acts
-    per_mirror = blocks // mirrors
-    surface = jnp.zeros((pup, pup), F32)
-    for m in range(mirrors):
-        part = jnp.concatenate([cmd_ref[m * per_mirror + j] for j in range(per_mirror)], axis=0)
-        for a in range(per_block):
-            act_ref[pl.ds(m * acts + a, per_mirror, stride=per_block), :acts] = part[:, a * acts : (a + 1) * acts]
-        actuators = act_ref[m * acts : (m + 1) * acts, :acts]
-        influence = infl_ref[m]
-        right = jnp.dot(actuators, influence, precision=HIGHEST, preferred_element_type=F32)
-        surface = surface + tdot(influence, right, HIGHEST)
-    height_ref[...] = aber_ref[...] + (2.0 * STROKE) * surface
-    place = (lax.broadcasted_iota(jnp.int32, (1, pup), 1).astype(F32) - (pup / 2 - 0.5)) * (1.0 / pup)
-    near = lax.broadcasted_iota(jnp.int32, (8, 1), 0).astype(F32) - (full / 2 - 0.5)
-    far = (lax.broadcasted_iota(jnp.int32, (full // 8, 1), 0) * 8).astype(F32)
     lane = lax.broadcasted_iota(jnp.int32, (1, LANES), 1)
-    band_at = pl.multiple_of(row * band, 16)
     mask = mask_ref[...]
     stat = jnp.zeros((1, LANES), F32)
+    near_u = lax.broadcasted_iota(jnp.int32, (8, 1), 0).astype(F32) - (full / 2 - 0.5)
+    far_u = (lax.broadcasted_iota(jnp.int32, (side // 8, 1), 0) * 8).astype(F32)
+    band_u = (lax.broadcasted_iota(jnp.int32, (band // 8, 1), 0) * 8 + row * band).astype(F32)
+    i = lax.broadcasted_iota(jnp.int32, (half, half), 0)
+    flip = (i + lax.broadcasted_iota(jnp.int32, (half, half), 1) == half - 1).astype(F32).astype(BF16)
+    i = lax.broadcasted_iota(jnp.int32, (2 * LANES, 2 * LANES), 0)
+    j = lax.broadcasted_iota(jnp.int32, (2 * LANES, 2 * LANES), 1)
+    back = ((i + j == full - 1 - LANES) & (i < side)).astype(F32).astype(BF16)
+    inverse = []
     for w in range(waves):
-        inverse = 1.0 / jnp.full((1, LANES), wave_ref[first_wave + w], F32)
-        inverse = jnp.concatenate([inverse] * (pup // LANES), axis=1)
-        cos, sin = cos_sin_turns(height_ref[...] * inverse)
+        one = 1.0 / jnp.full((1, LANES), wave_ref[first_wave + w], F32)
+        inverse.append(jnp.concatenate([one] * (pup // LANES), axis=1))
+
+    def pupil(w):
+        cos, sin = cos_sin_turns(height_ref[...] * inverse[w])
         amp = amp_ref[...]
-        pupil_hi, pupil_lo = split2(jnp.concatenate([amp * cos, amp * sin], axis=1))
-        turns = place * (PIXEL_SCALE * inverse)
-        near_c, near_s = cos_sin_turns(near * turns)
-        far_c, far_s = cos_sin_turns(far * turns)
-        for g in range(full // 8):
-            fc = far_c[g : g + 1]
-            fs = far_s[g : g + 1]
-            c = near_c * fc - near_s * fs
-            s = -(near_s * fc + near_c * fs)
-            rows8 = jnp.concatenate([c, s], axis=1)
-            hi = rows8.astype(BF16)
-            hi_ref[g * 8 : g * 8 + 8, :] = hi.astype(F32)
-            lo_ref[g * 8 : g * 8 + 8, :] = rows8 - hi.astype(F32)
-        y_hi = hi_ref[pl.ds(band_at, band), :].astype(BF16)
-        y_lo = lo_ref[pl.ds(band_at, band), :].astype(BF16)
-        y_hi = jnp.concatenate([y_hi[:, :pup], y_hi[:, pup:]], axis=0)
-        y_lo = jnp.concatenate([y_lo[:, :pup], y_lo[:, pup:]], axis=0)
-        up = mm(jnp.concatenate([y_hi, y_lo], axis=0), pupil_hi)
-        up = up[: 2 * band] + up[2 * band :] + mm(y_hi, pupil_lo)
-        mid_re = up[:band, :pup] - up[band:, pup:]
-        mid_im = up[:band, pup:] + up[band:, :pup]
-        mid_hi, mid_lo = split2(jnp.concatenate([mid_re, mid_im], axis=0))
-        both = jnp.concatenate([mid_hi, mid_lo], axis=0)
-        outs = []
-        for half in range(2):
-            x_hi = hi_ref[:, half * pup : (half + 1) * pup].astype(BF16)
-            x_lo = lo_ref[:, half * pup : (half + 1) * pup].astype(BF16)
-            o = mm_t(both, x_hi)
-            outs.append(o[: 2 * band] + o[2 * band :] + mm_t(mid_hi, x_lo))
-        re = outs[0][:band] - outs[1][band:]
-        im = outs[1][:band] + outs[0][band:]
-        intensity = re * re + im * im
+        return split2(jnp.concatenate([amp * cos, amp * sin], axis=0))
+
+    def band_table(w):
+        hi, lo = split2(transform(near_u, band_u, places(pup, pup) * (PIXEL_SCALE * inverse[w])))
+        return turned(hi), turned(lo)
+
+    def half_table(w):
+        return split2(transform(near_u, far_u, places(half, pup) * (PIXEL_SCALE * inverse[w][:, :half])))
+
+    def near_side(table, held):
+        pupil_hi, pupil_lo = held
+        y_hi, y_lo = table
+        return mm(jnp.concatenate([y_hi, y_lo], axis=0), pupil_hi), mm(y_hi, pupil_lo)
+
+    def fold(up, low):
+        up = up[: 2 * band] + up[2 * band :] + low
+        upper_hi, upper_lo = split2(up[:, half:])
+        return up[:, :half], mm(jnp.concatenate([upper_hi, upper_lo], axis=0), flip)
+
+    def middle(lower, upper):
+        upper = upper[: 2 * band] + upper[2 * band :]
+        parts = []
+        for even, odd in zip(split2(lower + upper), split2(lower - upper)):
+            re = even[:band]
+            im = even[band:]
+            odd_re = odd[:band]
+            odd_im = odd[band:]
+            rows = [(re, -odd_im), (im, odd_re), (re, odd_im), (im, -odd_re)]
+            rows = [jnp.concatenate(pair, axis=1) for pair in rows]
+            parts.append(jnp.concatenate(rows + [jnp.zeros((2 * LANES - 4 * band, pup), BF16)], axis=0))
+        return parts
+
+    def far_side(table, mid):
+        mid_hi, mid_lo = mid
+        hi, lo = table
+        return mm_t(hi, jnp.concatenate([mid_hi, mid_lo], axis=0)), mm_t(lo, mid_hi)
+
+    def unfold(field, low):
+        field = field[:, : 2 * LANES] + field[:, 2 * LANES :] + low
+        field = jnp.concatenate([field, jnp.zeros((2 * LANES - side, 2 * LANES), F32)], axis=0).T
+        field = field * field
+        far_hi, far_lo = split2(field[2 * band : 3 * band] + field[3 * band : 4 * band])
+        return field[:band] + field[band : 2 * band], mm(jnp.concatenate([far_hi, far_lo], axis=0), back)
+
+    def finish(w, near, far, stat):
+        far = far[:band] + far[band:]
+        intensity = jnp.concatenate([near[:, :LANES], near[:, LANES:] + far[:, :LANES], far[:, LANES:]], axis=1)
         out_ref[w] = intensity
         total = jnp.sum(jnp.sum(intensity, axis=0, keepdims=True), axis=1, keepdims=True)
         hole = jnp.sum(jnp.sum(intensity * mask, axis=0, keepdims=True), axis=1, keepdims=True)
         stat = jnp.where(lane == w, total, stat)
-        stat = jnp.where(lane == waves + w, hole, stat)
+        return jnp.where(lane == waves + w, hole, stat)
+
+    height_ref[...] = aber_ref[...] + (2.0 * STROKE) * mirror_surface(cmd_ref, infl_ref, half_refs)
+    first, folded, mid, field, image = {}, {}, {}, {}, {}
+    for step in range(waves + 4):
+        if step < waves:
+            first[step] = near_side(band_table(step), pupil(step))
+        w = step - 1
+        if 0 <= w < waves:
+            folded[w] = fold(*first.pop(w))
+        w = step - 2
+        if 0 <= w < waves:
+            field[w] = far_side(half_table(w), middle(*folded.pop(w)))
+        w = step - 3
+        if 0 <= w < waves:
+            image[w] = unfold(*field.pop(w))
+        w = step - 4
+        if 0 <= w < waves:
+            stat = finish(w, *image.pop(w), stat)
     spread(stat_ref, stat)
+    whole.wait()
 
 
 def scale_kernel(stat_ref, int_ref, out_ref, contrast_ref, *, holes):
@@ -255,13 +338,13 @@
         out_ref[w] = int_ref[w] * inverse[:, w : w + 1]
 
 
-def call(kernel, name, outs, args, scratch=(), smem=()):
+def call(kernel, name, outs, args, scratch=(), smem=(), hbm_out=()):
     return pl.pallas_call(
         kernel,
         out_shape=[jax.ShapeDtypeStruct(s, F32) for s in outs],
         in_specs=[pl.BlockSpec(memory_space=pltpu.SMEM if i in smem else pltpu.VMEM) for i in range(len(args))],
-        out_specs=[pl.BlockSpec(memory_space=pltpu.VMEM) for _ in outs],
-        scratch_shapes=[pltpu.VMEM(s, F32) for s in scratch],
+        out_specs=[pl.BlockSpec(memory_space=pl.ANY if i in hbm_out else pltpu.VMEM) for i in range(len(outs))],
+        scratch_shapes=[pltpu.VMEM(s, F32) if isinstance(s, tuple) else s for s in scratch],
         compiler_params=pltpu.CompilerParams(vmem_limit_bytes=16 << 20),
         cost_estimate=pl.CostEstimate(flops=20_000_000_000, bytes_accessed=1 << 20, transcendentals=0),
         name=name,
@@ -292,17 +375,17 @@
     grad = exchange(grad, "rows")
     (modal,) = call(modal_kernel, "modal", [(cols, 1, modes)], [grad, basis])
     modal = exchange(modal, "cols")
-    (parts,) = call(
-        command_kernel, "commands", [(rows, cands, width)],
-        [modal, eigenvalues, exponents, basis], smem=(2,),
+    (parts,) = call(command_kernel, "commands", [(rows, 1, LEVELS * width)], [modal, eigenvalues, basis])
+    parts = exchange(parts, "rows")
+    commands, chosen = call(
+        gather_kernel, "gather", [(cands, width), (cols, 1, width)], [parts, exponents],
+        scratch=[(1, LEVELS * width)], smem=(1,),
     )
-    parts = exchange(parts, "rows")
-    commands, chosen = call(gather_kernel, "gather", [(cands, width), (cols, 1, width)], [parts])
     chosen = exchange(chosen, "cols")
-    intensity, stat = call(
-        check_kernel, "check", [(waves, band, FP), (rows, 1, LANES)],
-        [chosen, jnp.swapaxes(influence, 1, 2), aberration, amplitude, wavelengths, mask],
-        scratch=[(2 * ACT, LANES), (PUP, PUP), (FP, 2 * PUP), (FP, 2 * PUP)], smem=(4,),
+    intensity, stat, commands = call(
+        check_kernel, "check", [(waves, band, FP), (rows, 1, LANES), (cands, width)],
+        [chosen, jnp.swapaxes(influence, 1, 2), aberration, amplitude, wavelengths, mask, commands],
+        scratch=check_scratch(waves), smem=(4,), hbm_out=(2,),
     )
     stat = exchange(stat, "rows")
     image, contrast = call(

time: 82.7 us -> 79.4 us (0.960)
  Pallas kernels: 13.7 us -> 11.1 us
    pallas_call x7, Pallas kernels: 13.7 us -> 11.1 us  [call(): pl.pallas_call(kernel, out_shape=[jax.ShapeDtypeStruct(s, F32) for s in o...]
where the time goes in v4:
time: 79.4 us; the launch traced here: 79 us
  blocking collectives  65.5 us (82%)
  Pallas kernels  11.1 us (14%)
  local copies, waits for them, and re-layouts  1.66 us (2%)
    all_to_all x6, blocking collectives, exchange(): return lax.all_to_all(x, axis, 0, 0)  65.5 us
    pallas_call x7, Pallas kernels, call(): pl.pallas_call(kernel, out_shape=[jax.ShapeDtypeStruct(s, F32) for s in o...  11.1 us
    unnamed x24, local copies, waits for them, and re-layouts  1.66 us

profile of v4, /device:TPU:1, one launch (start us, length us, event | category | flops | bytes accessed | tf_op | source)
XLA Modules:
  0.0 79.0 jit_solution(15132204454783355232)
XLA Ops:
  0.6 0.0 copy-start.4
  0.6 0.9 %copy-done.4 = f32[4,9216]{1,0:T(4,128)S(1)} copy-done((f32[4,9216]{1,0:T(4,128)S(1)}, f32[4,9216]{1,0:T(4,128)}, u32[]{:S(2)}) %copy-start.4) | copy-done | bytes 147480
  1.5 0.0 copy-start.5
  1.5 0.7 copy-done.5
  2.3 0.0 copy-start
  2.3 0.0 slice-start
  2.3 0.0 slice-start.1
  2.3 1.4 %pick.1 = (f32[16,1,2048]{2,1,0:T(1,128)S(1)}, f32[48,384]{1,0:T(8,128)S(1)}) custom-call(f32[4,9216]{1,0:T(4,128)S(1)} %copy-done.4, s32[1,4096]{1,0:T(1,128)S(1)} %bitcast.5), custom_call_target="tpu_custom_call" | custom-call | flops 20000000000 | bytes 1048576 | tf_op jit(solution)/shard_map/pick/pallas_call | solution.py:342
  3.7 14.5 %all_to_all.30.field_ref = f32[16,1,2048]{2,1,0:T(1,128)S(1)} all-to-all(f32[16,1,2048]{2,1,0:T(1,128)S(1)} %get-tuple-element.12), channel_id=1, replica_groups=mesh['rows'=8,'cols'=16] {'cols'}, dimensions={0} | all-to-all | bytes 262144 | tf_op jit(solution)/shard_map/all_to_all | solution.py:355
  18.2 0.0 copy-done
  18.2 0.8 gradient.1
  19.0 11.9 %all_to_all.31.grad_ref = f32[8,1,1152]{2,1,0:T(1,128)S(1)} all-to-all(f32[8,1,1152]{2,1,0:T(1,128)S(1)} %gradient.1), channel_id=1, replica_groups=mesh['rows'=8,'cols'=16] {'rows'}, dimensions={0} | all-to-all | bytes 73728 | tf_op jit(solution)/shard_map/all_to_all | solution.py:355
  30.9 0.0 slice-done
  30.9 0.0 slice-done.1
  30.9 0.0 slice-done.2
  30.9 0.0 copy-start.6
  30.9 0.8 modal.1
  31.7 9.8 %all_to_all.32.modal_ref = f32[16,1,2304]{2,1,0:T(1,128)S(1)} all-to-all(f32[16,1,2304]{2,1,0:T(1,128)S(1)} %modal.1), channel_id=1, replica_groups=mesh['rows'=8,'cols'=16] {'cols'}, dimensions={0} | all-to-all | bytes 294912 | tf_op jit(solution)/shard_map/all_to_all | solution.py:355
  41.5 0.0 copy-done.6
  41.5 2.0 %commands.1 = f32[8,1,6912]{2,1,0:T(1,128)S(1)} custom-call(f32[16,1,2304]{2,1,0:T(1,128)S(1)} %all_to_all.32.modal_ref, f32[2304]{0:T(1024)S(1)} %copy-done.6, f32[2304,1152]{1,0:T(8,128)S(1)} %bitcast.3), custom_call_target="tpu_custom_call" | custom-call | flops 20000000000 | bytes 1048576 | tf_op jit(solution)/shard_map/commands/pallas_call | solution.py:342
  43.5 10.6 %all_to_all.33.parts_ref = f32[8,1,6912]{2,1,0:T(1,128)S(1)} all-to-all(f32[8,1,6912]{2,1,0:T(1,128)S(1)} %commands.1), channel_id=1, replica_groups=mesh['rows'=8,'cols'=16] {'rows'}, dimensions={0} | all-to-all | bytes 442368 | tf_op jit(solution)/shard_map/all_to_all | solution.py:355
  54.1 0.0 copy-done.7
  54.1 0.0 copy-start.8
  54.1 0.6 gather.1
  54.7 9.3 %all_to_all.34.cmd_ref = f32[16,1,1152]{2,1,0:T(1,128)S(1)} all-to-all(f32[16,1,1152]{2,1,0:T(1,128)S(1)} %get-tuple-element.13), channel_id=1, replica_groups=mesh['rows'=8,'cols'=16] {'cols'}, dimensions={0} | all-to-all | bytes 147456 | tf_op jit(solution)/shard_map/all_to_all | solution.py:355
  64.0 0.0 copy-done.1
  64.0 0.0 copy-done.2
  64.0 0.0 copy-done.3
  64.0 0.0 copy-done.8
  64.1 4.7 %check.1 = (f32[6,48,384]{2,1,0:T(8,128)S(1)}, f32[8,1,128]{2,1,0:T(1,128)S(1)}, f32[8,1152]{1,0:T(8,128)}) custom-call(f32[16,1,1152]{2,1,0:T(1,128)S(1)} %all_to_all.34.cmd_ref, f32[2,96,256]{2,1,0:T(8,128)S(1)} %bitcast.4, f32[256,256]{1,0:T(8,128)S(1)} %copy-done.1, f32[256,256]{1,0:T(8,128)S(1)} %copy-done.2, f32[12]{0:T(128)S(1)} %copy-done.8, ...), custom_call_target="tpu_custom_call" | custom-call | flops 20000000000 | bytes 1048576 | tf_op jit(solution)/shard_map/check/pallas_call | solution.py:342
  68.8 9.3 %all_to_all.35.stat_ref = f32[8,1,128]{2,1,0:T(1,128)S(1)} all-to-all(f32[8,1,128]{2,1,0:T(1,128)S(1)} %get-tuple-element.17), channel_id=1, replica_groups=mesh['rows'=8,'cols'=16] {'rows'}, dimensions={0} | all-to-all | bytes 8192 | tf_op jit(solution)/shard_map/all_to_all | solution.py:355
  78.1 0.9 %scale.1 = (f32[6,48,384]{2,1,0:T(8,128)}, f32[1,6]{1,0:T(1,128)}) custom-call(f32[8,1,128]{2,1,0:T(1,128)S(1)} %all_to_all.35.stat_ref, f32[6,48,384]{2,1,0:T(8,128)S(1)} %get-tuple-element.18.int_ref), custom_call_target="tpu_custom_call" | custom-call | flops 20000000000 | bytes 1048576 | tf_op jit(solution)/shard_map/scale/pallas_call | solution.py:342
  (6 shorter events, 0.0 us)
Async XLA Ops:
  0.6 0.9 %copy-start.4 = (f32[4,9216]{1,0:T(4,128)S(1)}, f32[4,9216]{1,0:T(4,128)}, u32[]{:S(2)}) copy-start(f32[4,9216]{1,0:T(4,128)} %est_ref.1) | copy-start | bytes 442372
  1.5 0.7 copy-start.5
  2.3 15.9 %copy-start = (f32[2048,1152]{1,0:T(8,128)S(1)}, f32[2048,1152]{1,0:T(8,128)}, u32[]{:S(2)}) copy-start(f32[2048,1152]{1,0:T(8,128)} %jac_ref.1) | copy-start | bytes 28311556
  2.3 28.6 %slice-start = ((s8[10616832]{0:T(1024)(128)(4,1)}), s8[4194304]{0:T(1024)(128)(4,1)S(1)}, s32[]{:S(2)}) async-start(s8[10616832]{0:T(1024)(128)(4,1)} %bitcast.2), calls=%async_computation.6 | async-start | bytes 8388608
  2.3 28.6 %slice-start.1 = ((s8[10616832]{0:T(1024)(128)(4,1)}), s8[4194304]{0:T(1024)(128)(4,1)S(1)}, s32[]{:S(2)}) async-start(s8[10616832]{0:T(1024)(128)(4,1)} %bitcast.2), calls=%async_computation.7 | async-start | bytes 8388608
  18.2 12.7 %slice-start.2 = ((s8[10616832]{0:T(1024)(128)(4,1)}), s8[2228224]{0:T(1024)(128)(4,1)S(1)}, s32[]{:S(2)}) async-start(s8[10616832]{0:T(1024)(128)(4,1)} %bitcast.2), calls=%async_computation.8 | async-start | bytes 4456448
  30.9 10.6 %copy-start.6 = (f32[2304]{0:T(1024)S(1)}, f32[2304]{0:T(1024)}, u32[]{:S(2)}) copy-start(f32[2304]{0:T(1024)} %eig_ref.1) | copy-start | bytes 27652
  41.5 12.6 %copy-start.7 = (s32[8]{0:T(128)S(1)}, s32[8]{0:T(128)}, u32[]{:S(2)}) copy-start(s32[8]{0:T(128)} %exp_ref.1) | copy-start | bytes 100
  54.1 9.9 %copy-start.1 = (f32[256,256]{1,0:T(8,128)S(1)}, f32[256,256]{1,0:T(8,128)}, u32[]{:S(2)}) copy-start(f32[256,256]{1,0:T(8,128)} %aber_ref.1) | copy-start | bytes 786436
  54.1 9.9 %copy-start.2 = (f32[256,256]{1,0:T(8,128)S(1)}, f32[256,256]{1,0:T(8,128)}, u32[]{:S(2)}) copy-start(f32[256,256]{1,0:T(8,128)} %amp_ref.1) | copy-start | bytes 786436
  54.1 9.9 %copy-start.3 = (f32[2,256,96]{1,2,0:T(8,128)S(1)}, f32[2,256,96]{1,2,0:T(8,128)}, u32[]{:S(2)}) copy-start(f32[2,256,96]{1,2,0:T(8,128)} %param.19) | copy-start | bytes 589828
  54.1 9.9 %copy-start.8 = (f32[12]{0:T(128)S(1)}, f32[12]{0:T(128)}, u32[]{:S(2)}) copy-start(f32[12]{0:T(128)} %wave_ref.1) | copy-start | bytes 148

commit v5 on v4

--- a/solution.py
+++ b/solution.py
@@ -66,41 +66,45 @@
     return total
 
 
-def pick_kernel(est_ref, dh_ref, out_ref, mask_ref, table_ref, flat_ref):
+def reversal_kernel(flip_ref, back_ref):
+    half = flip_ref.shape[0]
+    wide = back_ref.shape[0]
+    i = lax.broadcasted_iota(jnp.int32, (half, half), 0)
+    j = lax.broadcasted_iota(jnp.int32, (half, half), 1)
+    flip_ref[...] = (i + j == half - 1).astype(F32).astype(BF16)
+    i = lax.broadcasted_iota(jnp.int32, (wide, wide), 0)
+    j = lax.broadcasted_iota(jnp.int32, (wide, wide), 1)
+    back_ref[...] = ((i + j == FP - 1 - (FP - wide)) & (i < FP // 2)).astype(F32).astype(BF16)
+
+
+def one_hot(rows, index):
+    held = jnp.clip(index, -1, 255).astype(F32).astype(BF16)
+    row = lax.broadcasted_iota(jnp.int32, (rows, 1), 0).astype(F32).astype(BF16)
+    return jnp.where(row == held, jnp.ones((), BF16), jnp.zeros((), BF16))
+
+
+def pick_kernel(est_ref, dh_ref, after_ref, out_ref, mask_ref, plane_ref, flat_ref):
     row = lax.axis_index("rows")
     col = lax.axis_index("cols")
-    rows = lax.axis_size("rows")
     planes, width = est_ref.shape
+    groups = width // LANES
     count = out_ref.shape[-1]
-    per_plane = rows // planes
-    plane = row // per_plane
+    per_plane = lax.axis_size("rows") // planes
     offset = pl.multiple_of((row % per_plane) * count, LANES)
-    groups = width // LANES
-    ours = lax.broadcasted_iota(jnp.int32, (planes, 1), 0) == plane
-    image = jnp.sum(jnp.where(ours, est_ref[...], 0.0), axis=0, keepdims=True)
+    ours = lax.broadcasted_iota(jnp.int32, (planes, 1), 0) == row // per_plane
+    plane = jnp.sum(jnp.where(ours, est_ref[...], 0.0), axis=0, keepdims=True)
     for j in range(groups):
-        table_ref[j : j + 1, :] = image[:, j * LANES : (j + 1) * LANES]
-    table = table_ref[...]
-    hi = table.astype(BF16)
-    rest = table - hi.astype(F32)
-    mid = rest.astype(BF16)
-    low = (rest - mid.astype(F32)).astype(BF16)
-    index = dh_ref[:, pl.ds(offset, count)]
-    place = index - col * width
-    group = place >> 7
-    lane = place & (LANES - 1)
-    one_hot = (lax.broadcasted_iota(jnp.int32, (groups, count), 0) == group).astype(F32).astype(BF16)
-    found = tdot(hi, one_hot) + tdot(mid, one_hot) + tdot(low, one_hot)
-    keep = lax.broadcasted_iota(jnp.int32, (LANES, count), 0) == lane
+        plane_ref[j : j + 1, :] = plane[:, j * LANES : (j + 1) * LANES]
+    hi, lo = split2(plane_ref[...])
+    place = dh_ref[:, pl.ds(offset, count)] - col * (groups * LANES)
+    chosen = one_hot(groups, place >> 7)
+    found = tdot(hi, chosen) + tdot(lo, chosen)
+    keep = lax.broadcasted_iota(jnp.int32, (LANES, count), 0) == (place & (LANES - 1))
     spread(out_ref, jnp.sum(jnp.where(keep, found, 0.0), axis=0, keepdims=True))
     band, full = mask_ref.shape
     per_row = full // LANES
     pix = dh_ref[...] - row * (band * full)
-    group = pix >> 7
-    lane = pix & (LANES - 1)
-    upper = (lax.broadcasted_iota(jnp.int32, (band * per_row, pix.shape[1]), 0) == group).astype(F32).astype(BF16)
-    lower = (lax.broadcasted_iota(jnp.int32, (LANES, pix.shape[1]), 0) == lane).astype(F32).astype(BF16)
-    flat_ref[...] = mm_t(upper, lower)
+    flat_ref[...] = mm_t(one_hot(band * per_row, pix >> 7), one_hot(LANES, pix & (LANES - 1)))
     for j in range(per_row):
         mask_ref[:, j * LANES : (j + 1) * LANES] = flat_ref[pl.ds(j, band, stride=per_row), :]
 
@@ -224,7 +228,7 @@
     return [pltpu.SemaphoreType.DMA, pltpu.VMEM((PUP, PUP), F32)] + [pltpu.VMEM((ACT, LANES), F32)] * 4
 
 
-def check_kernel(cmd_ref, infl_ref, aber_ref, amp_ref, wave_ref, mask_ref, all_ref, out_ref, stat_ref, all_out, sem, height_ref, *half_refs):
+def check_kernel(cmd_ref, infl_ref, aber_ref, amp_ref, wave_ref, mask_ref, all_ref, flip_ref, back_ref, out_ref, stat_ref, all_out, sem, height_ref, *half_refs):
     whole = pltpu.make_async_copy(all_ref, all_out, sem)
     whole.start()
     row = lax.axis_index("rows")
@@ -241,11 +245,8 @@
     near_u = lax.broadcasted_iota(jnp.int32, (8, 1), 0).astype(F32) - (full / 2 - 0.5)
     far_u = (lax.broadcasted_iota(jnp.int32, (side // 8, 1), 0) * 8).astype(F32)
     band_u = (lax.broadcasted_iota(jnp.int32, (band // 8, 1), 0) * 8 + row * band).astype(F32)
-    i = lax.broadcasted_iota(jnp.int32, (half, half), 0)
-    flip = (i + lax.broadcasted_iota(jnp.int32, (half, half), 1) == half - 1).astype(F32).astype(BF16)
-    i = lax.broadcasted_iota(jnp.int32, (2 * LANES, 2 * LANES), 0)
-    j = lax.broadcasted_iota(jnp.int32, (2 * LANES, 2 * LANES), 1)
-    back = ((i + j == full - 1 - LANES) & (i < side)).astype(F32).astype(BF16)
+    flip = flip_ref[...]
+    back = back_ref[...]
     inverse = []
     for w in range(waves):
         one = 1.0 / jnp.full((1, LANES), wave_ref[first_wave + w], F32)
@@ -338,11 +339,14 @@
         out_ref[w] = int_ref[w] * inverse[:, w : w + 1]
 
 
-def call(kernel, name, outs, args, scratch=(), smem=(), hbm_out=()):
+def call(kernel, name, outs, args, scratch=(), smem=(), hbm=(), hbm_out=()):
+    def space(i):
+        return pltpu.SMEM if i in smem else pl.ANY if i in hbm else pltpu.VMEM
+
     return pl.pallas_call(
         kernel,
-        out_shape=[jax.ShapeDtypeStruct(s, F32) for s in outs],
-        in_specs=[pl.BlockSpec(memory_space=pltpu.SMEM if i in smem else pltpu.VMEM) for i in range(len(args))],
+        out_shape=[jax.ShapeDtypeStruct(s, F32) if isinstance(s, tuple) else s for s in outs],
+        in_specs=[pl.BlockSpec(memory_space=space(i)) for i in range(len(args))],
         out_specs=[pl.BlockSpec(memory_space=pl.ANY if i in hbm_out else pltpu.VMEM) for i in range(len(outs))],
         scratch_shapes=[pltpu.VMEM(s, F32) if isinstance(s, tuple) else s for s in scratch],
         compiler_params=pltpu.CompilerParams(vmem_limit_bytes=16 << 20),
@@ -364,11 +368,12 @@
     waves = wavelengths.shape[0] // (cols // cands)
     band = FP // rows
     holes = dark_hole.shape[0]
-    groups = estimate.shape[1] // LANES
+    square = [jax.ShapeDtypeStruct((n, n), BF16) for n in (PUP // 2, 2 * LANES)]
+    flip, back = call(reversal_kernel, "reversals", square, [])
     share, mask = call(
         pick_kernel, "pick", [(cols, 1, tile_rows), (band, FP)],
-        [estimate, dark_hole.reshape(1, holes)],
-        scratch=[(groups, LANES), (band * FP // LANES, LANES)],
+        [estimate, dark_hole.reshape(1, holes), flip],
+        scratch=[(estimate.shape[1] // LANES, LANES), (band * FP // LANES, LANES)], hbm=(2,),
     )
     share = exchange(share, "cols")
     (grad,) = call(gradient_kernel, "gradient", [(rows, 1, width)], [share, jacobian])
@@ -384,7 +389,7 @@
     chosen = exchange(chosen, "cols")
     intensity, stat, commands = call(
         check_kernel, "check", [(waves, band, FP), (rows, 1, LANES), (cands, width)],
-        [chosen, jnp.swapaxes(influence, 1, 2), aberration, amplitude, wavelengths, mask, commands],
+        [chosen, jnp.swapaxes(influence, 1, 2), aberration, amplitude, wavelengths, mask, commands, flip, back],
         scratch=check_scratch(waves), smem=(4,), hbm_out=(2,),
     )
     stat = exchange(stat, "rows")

time: 79.4 us -> 78.3 us (0.986)
    unnamed x24 -> x28, local copies, waits for them, and re-layouts: 1.66 us -> 0.91 us
    pallas_call x7 -> x8, Pallas kernels: 11.1 us -> 10.7 us  [call(): pl.pallas_call(kernel, out_shape=[jax.ShapeDtypeStruct(s, F32) if isinsta...]
where the time goes in v5:
time: 78.3 us; the launch traced here: 77.9 us
  blocking collectives  65.5 us (84%)
  Pallas kernels  10.7 us (14%)
  local copies, waits for them, and re-layouts  0.91 us (1%)
    all_to_all x6, blocking collectives, exchange(): return lax.all_to_all(x, axis, 0, 0)  65.5 us
    pallas_call x8, Pallas kernels, call(): pl.pallas_call(kernel, out_shape=[jax.ShapeDtypeStruct(s, F32) if isinsta...  10.7 us

profile of v5, /device:TPU:1, one launch (start us, length us, event | category | flops | bytes accessed | tf_op | source)
XLA Modules:
  0.0 77.9 jit_solution(308462635677342660)
XLA Ops:
  0.6 0.0 copy-start.4
  0.6 0.0 copy-start.3
  0.6 0.0 slice-start.3
  0.7 0.0 slice-start.4
  0.7 0.6 copy-done.4
  1.3 0.2 copy-done.3
  1.6 1.0 %pick.1 = (f32[16,1,2048]{2,1,0:T(1,128)S(1)}, f32[48,384]{1,0:T(8,128)S(1)}) custom-call(f32[4,9216]{1,0:T(4,128)S(1)} %copy-done.3, s32[1,4096]{1,0:T(1,128)S(1)} %bitcast.7, bf16[128,128]{1,0:T(8,128)(2,1)S(1)} %get-tuple-element.14.after_ref.flip_ref), custom_call_target="tpu_custom_call" | custom-call | flops 20000000000 | bytes 1048576 | tf_op jit(solution)/shard_map/pick/pallas_call | solution.py:346
  2.5 14.5 %all_to_all.30.field_ref = f32[16,1,2048]{2,1,0:T(1,128)S(1)} all-to-all(f32[16,1,2048]{2,1,0:T(1,128)S(1)} %get-tuple-element.15), channel_id=1, replica_groups=mesh['rows'=8,'cols'=16] {'cols'}, dimensions={0} | all-to-all | bytes 262144 | tf_op jit(solution)/shard_map/all_to_all | solution.py:359
  17.0 0.0 slice-done.3
  17.0 0.0 slice-done.4
  17.0 0.0 slice-done.5
  17.1 0.0 slice-start.2
  17.1 0.8 %gradient.1 = f32[8,1,1152]{2,1,0:T(1,128)S(1)} custom-call(f32[16,1,2048]{2,1,0:T(1,128)S(1)} %all_to_all.30.field_ref, f32[2048,1152]{1,0:T(8,128)S(1)} %bitcast.5), custom_call_target="tpu_custom_call" | custom-call | flops 20000000000 | bytes 1048576 | tf_op jit(solution)/shard_map/gradient/pallas_call | solution.py:346
  17.9 11.9 %all_to_all.31.grad_ref = f32[8,1,1152]{2,1,0:T(1,128)S(1)} all-to-all(f32[8,1,1152]{2,1,0:T(1,128)S(1)} %gradient.1), channel_id=1, replica_groups=mesh['rows'=8,'cols'=16] {'rows'}, dimensions={0} | all-to-all | bytes 73728 | tf_op jit(solution)/shard_map/all_to_all | solution.py:359
  29.8 0.0 slice-done
  29.8 0.0 slice-done.1
  29.8 0.0 slice-done.2
  29.8 0.0 copy-start.5
  29.8 0.8 modal.1
  30.6 9.8 %all_to_all.32.modal_ref = f32[16,1,2304]{2,1,0:T(1,128)S(1)} all-to-all(f32[16,1,2304]{2,1,0:T(1,128)S(1)} %modal.1), channel_id=1, replica_groups=mesh['rows'=8,'cols'=16] {'cols'}, dimensions={0} | all-to-all | bytes 294912 | tf_op jit(solution)/shard_map/all_to_all | solution.py:359
  40.4 0.0 copy-done.5
  40.4 2.0 %commands.1 = f32[8,1,6912]{2,1,0:T(1,128)S(1)} custom-call(f32[16,1,2304]{2,1,0:T(1,128)S(1)} %all_to_all.32.modal_ref, f32[2304]{0:T(1024)S(1)} %copy-done.5, f32[2304,1152]{1,0:T(8,128)S(1)} %bitcast.3), custom_call_target="tpu_custom_call" | custom-call | flops 20000000000 | bytes 1048576 | tf_op jit(solution)/shard_map/commands/pallas_call | solution.py:346
  42.4 10.6 %all_to_all.33.parts_ref = f32[8,1,6912]{2,1,0:T(1,128)S(1)} all-to-all(f32[8,1,6912]{2,1,0:T(1,128)S(1)} %commands.1), channel_id=1, replica_groups=mesh['rows'=8,'cols'=16] {'rows'}, dimensions={0} | all-to-all | bytes 442368 | tf_op jit(solution)/shard_map/all_to_all | solution.py:359
  53.0 0.0 copy-done.6
  53.0 0.0 copy-start.7
  53.0 0.6 gather.1
  53.6 9.3 %all_to_all.34.cmd_ref = f32[16,1,1152]{2,1,0:T(1,128)S(1)} all-to-all(f32[16,1,1152]{2,1,0:T(1,128)S(1)} %get-tuple-element.16), channel_id=1, replica_groups=mesh['rows'=8,'cols'=16] {'cols'}, dimensions={0} | all-to-all | bytes 147456 | tf_op jit(solution)/shard_map/all_to_all | solution.py:359
  62.9 0.0 copy-done
  62.9 0.0 copy-done.1
  63.0 4.7 %check.1 = (f32[6,48,384]{2,1,0:T(8,128)S(1)}, f32[8,1,128]{2,1,0:T(1,128)S(1)}, f32[8,1152]{1,0:T(8,128)}) custom-call(f32[16,1,1152]{2,1,0:T(1,128)S(1)} %all_to_all.34.cmd_ref, f32[2,96,256]{2,1,0:T(8,128)S(1)} %bitcast.6, f32[256,256]{1,0:T(8,128)S(1)} %copy-done, f32[256,256]{1,0:T(8,128)S(1)} %copy-done.1, f32[12]{0:T(128)S(1)} %copy-done.7, ...), custom_call_target="tpu_custom_call" | custom-call | flops 20000000000 | bytes 1048576 | tf_op jit(solution)/shard_map/check/pallas_call | solution.py:346
  67.7 9.3 %all_to_all.35.stat_ref = f32[8,1,128]{2,1,0:T(1,128)S(1)} all-to-all(f32[8,1,128]{2,1,0:T(1,128)S(1)} %get-tuple-element.21), channel_id=1, replica_groups=mesh['rows'=8,'cols'=16] {'rows'}, dimensions={0} | all-to-all | bytes 8192 | tf_op jit(solution)/shard_map/all_to_all | solution.py:359
  77.0 0.9 %scale.1 = (f32[6,48,384]{2,1,0:T(8,128)}, f32[1,6]{1,0:T(1,128)}) custom-call(f32[8,1,128]{2,1,0:T(1,128)S(1)} %all_to_all.35.stat_ref, f32[6,48,384]{2,1,0:T(8,128)S(1)} %get-tuple-element.22.int_ref), custom_call_target="tpu_custom_call" | custom-call | flops 20000000000 | bytes 1048576 | tf_op jit(solution)/shard_map/scale/pallas_call | solution.py:346
  (12 shorter events, 0.0 us)
Async XLA Ops:
  0.6 0.7 copy-start.4
  0.6 0.9 %copy-start.3 = (f32[4,9216]{1,0:T(4,128)S(1)}, f32[4,9216]{1,0:T(4,128)}, u32[]{:S(2)}) copy-start(f32[4,9216]{1,0:T(4,128)} %est_ref.1) | copy-start | bytes 442372
  0.6 16.4 %slice-start.3 = ((s8[9437184]{0:T(1024)(128)(4,1)}), s8[4194304]{0:T(1024)(128)(4,1)S(1)}, s32[]{:S(2)}) async-start(s8[9437184]{0:T(1024)(128)(4,1)} %bitcast.4), calls=%async_computation.9 | async-start | bytes 8388608
  0.7 16.4 %slice-start.4 = ((s8[9437184]{0:T(1024)(128)(4,1)}), s8[4194304]{0:T(1024)(128)(4,1)S(1)}, s32[]{:S(2)}) async-start(s8[9437184]{0:T(1024)(128)(4,1)} %bitcast.4), calls=%async_computation.10 | async-start | bytes 8388608
  1.6 15.5 %slice-start.5 = ((s8[9437184]{0:T(1024)(128)(4,1)}), s8[1048576]{0:T(1024)(128)(4,1)S(1)}, s32[]{:S(2)}) async-start(s8[9437184]{0:T(1024)(128)(4,1)} %bitcast.4), calls=%async_computation.11 | async-start | bytes 2097152
  1.6 28.2 %slice-start = ((s8[10616832]{0:T(1024)(128)(4,1)}), s8[4194304]{0:T(1024)(128)(4,1)S(1)}, s32[]{:S(2)}) async-start(s8[10616832]{0:T(1024)(128)(4,1)} %bitcast.2), calls=%async_computation.6 | async-start | bytes 8388608
  1.6 28.2 %slice-start.1 = ((s8[10616832]{0:T(1024)(128)(4,1)}), s8[4194304]{0:T(1024)(128)(4,1)S(1)}, s32[]{:S(2)}) async-start(s8[10616832]{0:T(1024)(128)(4,1)} %bitcast.2), calls=%async_computation.7 | async-start | bytes 8388608
  17.1 12.7 %slice-start.2 = ((s8[10616832]{0:T(1024)(128)(4,1)}), s8[2228224]{0:T(1024)(128)(4,1)S(1)}, s32[]{:S(2)}) async-start(s8[10616832]{0:T(1024)(128)(4,1)} %bitcast.2), calls=%async_computation.8 | async-start | bytes 4456448
  29.8 10.6 %copy-start.5 = (f32[2304]{0:T(1024)S(1)}, f32[2304]{0:T(1024)}, u32[]{:S(2)}) copy-start(f32[2304]{0:T(1024)} %eig_ref.1) | copy-start | bytes 27652
  40.4 12.6 %copy-start.6 = (s32[8]{0:T(128)S(1)}, s32[8]{0:T(128)}, u32[]{:S(2)}) copy-start(s32[8]{0:T(128)} %exp_ref.1) | copy-start | bytes 100
  53.0 9.9 %copy-start = (f32[256,256]{1,0:T(8,128)S(1)}, f32[256,256]{1,0:T(8,128)}, u32[]{:S(2)}) copy-start(f32[256,256]{1,0:T(8,128)} %aber_ref.1) | copy-start | bytes 786436
  53.0 9.9 %copy-start.1 = (f32[256,256]{1,0:T(8,128)S(1)}, f32[256,256]{1,0:T(8,128)}, u32[]{:S(2)}) copy-start(f32[256,256]{1,0:T(8,128)} %amp_ref.1) | copy-start | bytes 786436
  53.0 9.9 %copy-start.2 = (f32[2,256,96]{1,2,0:T(8,128)S(1)}, f32[2,256,96]{1,2,0:T(8,128)}, u32[]{:S(2)}) copy-start(f32[2,256,96]{1,2,0:T(8,128)} %param.19) | copy-start | bytes 589828
  53.0 9.9 %copy-start.7 = (f32[12]{0:T(128)S(1)}, f32[12]{0:T(128)}, u32[]{:S(2)}) copy-start(f32[12]{0:T(128)} %wave_ref.1) | copy-start | bytes 148

commit v6 on v5

--- a/solution.py
+++ b/solution.py
@@ -59,6 +59,14 @@
         ref[j] = row
 
 
+def spread_rows(ref, row):
+    for b in range(ref.shape[1]):
+        ref[0, b : b + 1, :] = row[:, b * LANES : (b + 1) * LANES]
+    block = ref[0]
+    for j in range(1, ref.shape[0]):
+        ref[j] = block
+
+
 def gathered_sum(ref):
     total = ref[0]
     for j in range(1, ref.shape[0]):
@@ -68,13 +76,13 @@
 
 def reversal_kernel(flip_ref, back_ref):
     half = flip_ref.shape[0]
-    wide = back_ref.shape[0]
+    side, wide = back_ref.shape
     i = lax.broadcasted_iota(jnp.int32, (half, half), 0)
     j = lax.broadcasted_iota(jnp.int32, (half, half), 1)
     flip_ref[...] = (i + j == half - 1).astype(F32).astype(BF16)
-    i = lax.broadcasted_iota(jnp.int32, (wide, wide), 0)
-    j = lax.broadcasted_iota(jnp.int32, (wide, wide), 1)
-    back_ref[...] = ((i + j == FP - 1 - (FP - wide)) & (i < FP // 2)).astype(F32).astype(BF16)
+    i = lax.broadcasted_iota(jnp.int32, (side, wide), 0)
+    j = lax.broadcasted_iota(jnp.int32, (side, wide), 1)
+    back_ref[...] = (i + j == wide - 1).astype(F32).astype(BF16)
 
 
 def one_hot(rows, index):
@@ -159,19 +167,24 @@
         hi, lo = split2(basis_ref[at, :])
         acc = acc + mm(both, hi) + mm(both, lo)
     levels = acc[:rows] + acc[rows:]
-    spread(out_ref, jnp.concatenate([levels[l : l + 1] for l in range(LEVELS)], axis=1))
+    spread_rows(out_ref, jnp.concatenate([levels[l : l + 1] for l in range(LEVELS)], axis=1))
 
 
 def gather_kernel(parts_ref, exp_ref, out_ref, send_ref, levels_ref):
-    levels_ref[...] = gathered_sum(parts_ref)
+    total = gathered_sum(parts_ref)
+    for b in range(levels_ref.shape[0]):
+        levels_ref[b] = total[b : b + 1]
     cands, width = out_ref.shape
     copies = send_ref.shape[0] // cands
+    tiles = width // LANES
     for k in range(cands):
-        level = exp_ref[k] - LEAST
-        row = levels_ref[:, pl.ds(pl.multiple_of(level * width, LANES), width)]
-        out_ref[k : k + 1, :] = row
-        for j in range(copies):
-            send_ref[k * copies + j] = row
+        start = (exp_ref[k] - LEAST) * tiles
+        for t in range(tiles):
+            piece = levels_ref[start + t]
+            at = slice(t * LANES, (t + 1) * LANES)
+            out_ref[k : k + 1, at] = piece
+            for j in range(copies):
+                send_ref[k * copies + j, :, at] = piece
 
 
 def transform(near_u, far_u, turns):
@@ -283,21 +296,21 @@
             odd_re = odd[:band]
             odd_im = odd[band:]
             rows = [(re, -odd_im), (im, odd_re), (re, odd_im), (im, -odd_re)]
-            rows = [jnp.concatenate(pair, axis=1) for pair in rows]
-            parts.append(jnp.concatenate(rows + [jnp.zeros((2 * LANES - 4 * band, pup), BF16)], axis=0))
+            parts.append(jnp.concatenate([jnp.concatenate(pair, axis=1) for pair in rows], axis=0))
         return parts
 
     def far_side(table, mid):
         mid_hi, mid_lo = mid
         hi, lo = table
-        return mm_t(hi, jnp.concatenate([mid_hi, mid_lo], axis=0)), mm_t(lo, mid_hi)
+        return mm_t(jnp.concatenate([mid_hi, mid_lo], axis=0), hi), mm_t(mid_hi, lo)
 
     def unfold(field, low):
-        field = field[:, : 2 * LANES] + field[:, 2 * LANES :] + low
-        field = jnp.concatenate([field, jnp.zeros((2 * LANES - side, 2 * LANES), F32)], axis=0).T
+        field = field[: 4 * band] + field[4 * band :] + low
         field = field * field
-        far_hi, far_lo = split2(field[2 * band : 3 * band] + field[3 * band : 4 * band])
-        return field[:band] + field[band : 2 * band], mm(jnp.concatenate([far_hi, far_lo], axis=0), back)
+        near = field[:band] + field[band : 2 * band]
+        near = jnp.concatenate([near, jnp.zeros((band, 2 * LANES - side), F32)], axis=1)
+        far_hi, far_lo = split2(field[2 * band : 3 * band] + field[3 * band :])
+        return near, mm(jnp.concatenate([far_hi, far_lo], axis=0), back)
 
     def finish(w, near, far, stat):
         far = far[:band] + far[band:]
@@ -368,8 +381,8 @@
     waves = wavelengths.shape[0] // (cols // cands)
     band = FP // rows
     holes = dark_hole.shape[0]
-    square = [jax.ShapeDtypeStruct((n, n), BF16) for n in (PUP // 2, 2 * LANES)]
-    flip, back = call(reversal_kernel, "reversals", square, [])
+    matrices = [jax.ShapeDtypeStruct(s, BF16) for s in ((PUP // 2, PUP // 2), (FP // 2, 2 * LANES))]
+    flip, back = call(reversal_kernel, "reversals", matrices, [])
     share, mask = call(
         pick_kernel, "pick", [(cols, 1, tile_rows), (band, FP)],
         [estimate, dark_hole.reshape(1, holes), flip],
@@ -380,11 +393,11 @@
     grad = exchange(grad, "rows")
     (modal,) = call(modal_kernel, "modal", [(cols, 1, modes)], [grad, basis])
     modal = exchange(modal, "cols")
-    (parts,) = call(command_kernel, "commands", [(rows, 1, LEVELS * width)], [modal, eigenvalues, basis])
+    (parts,) = call(command_kernel, "commands", [(rows, LEVELS * width // LANES, LANES)], [modal, eigenvalues, basis])
     parts = exchange(parts, "rows")
     commands, chosen = call(
         gather_kernel, "gather", [(cands, width), (cols, 1, width)], [parts, exponents],
-        scratch=[(1, LEVELS * width)], smem=(1,),
+        scratch=[(LEVELS * width // LANES, 1, LANES)], smem=(1,),
     )
     chosen = exchange(chosen, "cols")
     intensity, stat, commands = call(

time: 78.3 us -> 78.2 us (level)
  no operation moved by 1% of the time
where the time goes in v6:
time: 78.2 us; the launch traced here: 77.8 us
  blocking collectives  65.6 us (84%)
  Pallas kernels  10.5 us (13%)
  local copies, waits for them, and re-layouts  0.91 us (1%)
    all_to_all x6, blocking collectives, exchange(): return lax.all_to_all(x, axis, 0, 0)  65.6 us
    pallas_call x8, Pallas kernels, call(): pl.pallas_call(kernel, out_shape=[jax.ShapeDtypeStruct(s, F32) if isinsta...  10.5 us

profile of v6, /device:TPU:1, one launch (start us, length us, event | category | flops | bytes accessed | tf_op | source)
XLA Modules:
  0.0 77.8 jit_solution(2860922239596609199)
XLA Ops:
  0.6 0.0 copy-start.4
  0.6 0.0 copy-start.3
  0.6 0.0 slice-start.3
  0.7 0.0 slice-start.4
  0.7 0.6 copy-done.4
  1.3 0.2 copy-done.3
  1.6 1.0 %pick.1 = (f32[16,1,2048]{2,1,0:T(1,128)S(1)}, f32[48,384]{1,0:T(8,128)S(1)}) custom-call(f32[4,9216]{1,0:T(4,128)S(1)} %copy-done.3, s32[1,4096]{1,0:T(1,128)S(1)} %bitcast.7, bf16[128,128]{1,0:T(8,128)(2,1)S(1)} %get-tuple-element.14.after_ref.flip_ref), custom_call_target="tpu_custom_call" | custom-call | flops 20000000000 | bytes 1048576 | tf_op jit(solution)/shard_map/pick/pallas_call | solution.py:359
  2.5 14.5 %all_to_all.30.field_ref = f32[16,1,2048]{2,1,0:T(1,128)S(1)} all-to-all(f32[16,1,2048]{2,1,0:T(1,128)S(1)} %get-tuple-element.15), channel_id=1, replica_groups=mesh['rows'=8,'cols'=16] {'cols'}, dimensions={0} | all-to-all | bytes 262144 | tf_op jit(solution)/shard_map/all_to_all | solution.py:372
  17.0 0.0 slice-done.3
  17.0 0.0 slice-done.4
  17.0 0.0 slice-done.5
  17.1 0.0 slice-start.2
  17.1 0.8 %gradient.1 = f32[8,1,1152]{2,1,0:T(1,128)S(1)} custom-call(f32[16,1,2048]{2,1,0:T(1,128)S(1)} %all_to_all.30.field_ref, f32[2048,1152]{1,0:T(8,128)S(1)} %bitcast.5), custom_call_target="tpu_custom_call" | custom-call | flops 20000000000 | bytes 1048576 | tf_op jit(solution)/shard_map/gradient/pallas_call | solution.py:359
  17.9 11.9 %all_to_all.31.grad_ref = f32[8,1,1152]{2,1,0:T(1,128)S(1)} all-to-all(f32[8,1,1152]{2,1,0:T(1,128)S(1)} %gradient.1), channel_id=1, replica_groups=mesh['rows'=8,'cols'=16] {'rows'}, dimensions={0} | all-to-all | bytes 73728 | tf_op jit(solution)/shard_map/all_to_all | solution.py:372
  29.8 0.0 slice-done
  29.8 0.0 slice-done.1
  29.8 0.0 slice-done.2
  29.8 0.0 copy-start.5
  29.8 0.8 modal.1
  30.6 9.8 %all_to_all.32.modal_ref = f32[16,1,2304]{2,1,0:T(1,128)S(1)} all-to-all(f32[16,1,2304]{2,1,0:T(1,128)S(1)} %modal.1), channel_id=1, replica_groups=mesh['rows'=8,'cols'=16] {'cols'}, dimensions={0} | all-to-all | bytes 294912 | tf_op jit(solution)/shard_map/all_to_all | solution.py:372
  40.4 0.0 copy-done.5
  40.4 2.0 %commands.1 = f32[8,54,128]{2,1,0:T(8,128)S(1)} custom-call(f32[16,1,2304]{2,1,0:T(1,128)S(1)} %all_to_all.32.modal_ref, f32[2304]{0:T(1024)S(1)} %copy-done.5, f32[2304,1152]{1,0:T(8,128)S(1)} %bitcast.3), custom_call_target="tpu_custom_call" | custom-call | flops 20000000000 | bytes 1048576 | tf_op jit(solution)/shard_map/commands/pallas_call | solution.py:359
  42.4 10.7 %all_to_all.33.parts_ref = f32[8,54,128]{2,1,0:T(8,128)S(1)} all-to-all(f32[8,54,128]{2,1,0:T(8,128)S(1)} %commands.1), channel_id=1, replica_groups=mesh['rows'=8,'cols'=16] {'rows'}, dimensions={0} | all-to-all | bytes 442368 | tf_op jit(solution)/shard_map/all_to_all | solution.py:372
  53.1 0.0 copy-done.6
  53.1 0.0 copy-start.7
  53.1 0.6 gather.1
  53.7 9.3 %all_to_all.34.cmd_ref = f32[16,1,1152]{2,1,0:T(1,128)S(1)} all-to-all(f32[16,1,1152]{2,1,0:T(1,128)S(1)} %get-tuple-element.16), channel_id=1, replica_groups=mesh['rows'=8,'cols'=16] {'cols'}, dimensions={0} | all-to-all | bytes 147456 | tf_op jit(solution)/shard_map/all_to_all | solution.py:372
  63.1 0.0 copy-done
  63.1 0.0 copy-done.7
  63.1 4.5 %check.1 = (f32[6,48,384]{2,1,0:T(8,128)S(1)}, f32[8,1,128]{2,1,0:T(1,128)S(1)}, f32[8,1152]{1,0:T(8,128)}) custom-call(f32[16,1,1152]{2,1,0:T(1,128)S(1)} %all_to_all.34.cmd_ref, f32[2,96,256]{2,1,0:T(8,128)S(1)} %bitcast.6, f32[256,256]{1,0:T(8,128)S(1)} %copy-done, f32[256,256]{1,0:T(8,128)S(1)} %copy-done.1, f32[12]{0:T(128)S(1)} %copy-done.7, ...), custom_call_target="tpu_custom_call" | custom-call | flops 20000000000 | bytes 1048576 | tf_op jit(solution)/shard_map/check/pallas_call | solution.py:359
  67.6 9.3 %all_to_all.35.stat_ref = f32[8,1,128]{2,1,0:T(1,128)S(1)} all-to-all(f32[8,1,128]{2,1,0:T(1,128)S(1)} %get-tuple-element.21), channel_id=1, replica_groups=mesh['rows'=8,'cols'=16] {'rows'}, dimensions={0} | all-to-all | bytes 8192 | tf_op jit(solution)/shard_map/all_to_all | solution.py:372
  76.9 0.9 %scale.1 = (f32[6,48,384]{2,1,0:T(8,128)}, f32[1,6]{1,0:T(1,128)}) custom-call(f32[8,1,128]{2,1,0:T(1,128)S(1)} %all_to_all.35.stat_ref, f32[6,48,384]{2,1,0:T(8,128)S(1)} %get-tuple-element.22.int_ref), custom_call_target="tpu_custom_call" | custom-call | flops 20000000000 | bytes 1048576 | tf_op jit(solution)/shard_map/scale/pallas_call | solution.py:359
  (12 shorter events, 0.0 us)
Async XLA Ops:
  0.6 0.7 copy-start.4
  0.6 0.9 %copy-start.3 = (f32[4,9216]{1,0:T(4,128)S(1)}, f32[4,9216]{1,0:T(4,128)}, u32[]{:S(2)}) copy-start(f32[4,9216]{1,0:T(4,128)} %est_ref.1) | copy-start | bytes 442372
  0.6 16.4 %slice-start.3 = ((s8[9437184]{0:T(1024)(128)(4,1)}), s8[4194304]{0:T(1024)(128)(4,1)S(1)}, s32[]{:S(2)}) async-start(s8[9437184]{0:T(1024)(128)(4,1)} %bitcast.4), calls=%async_computation.9 | async-start | bytes 8388608
  0.7 16.4 %slice-start.4 = ((s8[9437184]{0:T(1024)(128)(4,1)}), s8[4194304]{0:T(1024)(128)(4,1)S(1)}, s32[]{:S(2)}) async-start(s8[9437184]{0:T(1024)(128)(4,1)} %bitcast.4), calls=%async_computation.10 | async-start | bytes 8388608
  1.6 15.5 %slice-start.5 = ((s8[9437184]{0:T(1024)(128)(4,1)}), s8[1048576]{0:T(1024)(128)(4,1)S(1)}, s32[]{:S(2)}) async-start(s8[9437184]{0:T(1024)(128)(4,1)} %bitcast.4), calls=%async_computation.11 | async-start | bytes 2097152
  1.6 28.2 %slice-start = ((s8[10616832]{0:T(1024)(128)(4,1)}), s8[4194304]{0:T(1024)(128)(4,1)S(1)}, s32[]{:S(2)}) async-start(s8[10616832]{0:T(1024)(128)(4,1)} %bitcast.2), calls=%async_computation.6 | async-start | bytes 8388608
  1.6 28.2 %slice-start.1 = ((s8[10616832]{0:T(1024)(128)(4,1)}), s8[4194304]{0:T(1024)(128)(4,1)S(1)}, s32[]{:S(2)}) async-start(s8[10616832]{0:T(1024)(128)(4,1)} %bitcast.2), calls=%async_computation.7 | async-start | bytes 8388608
  17.1 12.7 %slice-start.2 = ((s8[10616832]{0:T(1024)(128)(4,1)}), s8[2228224]{0:T(1024)(128)(4,1)S(1)}, s32[]{:S(2)}) async-start(s8[10616832]{0:T(1024)(128)(4,1)} %bitcast.2), calls=%async_computation.8 | async-start | bytes 4456448
  29.8 10.6 %copy-start.5 = (f32[2304]{0:T(1024)S(1)}, f32[2304]{0:T(1024)}, u32[]{:S(2)}) copy-start(f32[2304]{0:T(1024)} %eig_ref.1) | copy-start | bytes 27652
  40.4 12.7 %copy-start.6 = (s32[8]{0:T(128)S(1)}, s32[8]{0:T(128)}, u32[]{:S(2)}) copy-start(s32[8]{0:T(128)} %exp_ref.1) | copy-start | bytes 100
  53.1 10.0 %copy-start = (f32[256,256]{1,0:T(8,128)S(1)}, f32[256,256]{1,0:T(8,128)}, u32[]{:S(2)}) copy-start(f32[256,256]{1,0:T(8,128)} %aber_ref.1) | copy-start | bytes 786436
  53.1 10.0 %copy-start.1 = (f32[256,256]{1,0:T(8,128)S(1)}, f32[256,256]{1,0:T(8,128)}, u32[]{:S(2)}) copy-start(f32[256,256]{1,0:T(8,128)} %amp_ref.1) | copy-start | bytes 786436
  53.1 10.0 %copy-start.2 = (f32[2,256,96]{1,2,0:T(8,128)S(1)}, f32[2,256,96]{1,2,0:T(8,128)}, u32[]{:S(2)}) copy-start(f32[2,256,96]{1,2,0:T(8,128)} %param.19) | copy-start | bytes 589828
  53.1 10.0 %copy-start.7 = (f32[12]{0:T(128)S(1)}, f32[12]{0:T(128)}, u32[]{:S(2)}) copy-start(f32[12]{0:T(128)} %wave_ref.1) | copy-start | bytes 148

commit v7 on v5

--- a/solution.py
+++ b/solution.py
@@ -68,13 +68,13 @@
 
 def reversal_kernel(flip_ref, back_ref):
     half = flip_ref.shape[0]
-    wide = back_ref.shape[0]
+    side, wide = back_ref.shape
     i = lax.broadcasted_iota(jnp.int32, (half, half), 0)
     j = lax.broadcasted_iota(jnp.int32, (half, half), 1)
     flip_ref[...] = (i + j == half - 1).astype(F32).astype(BF16)
-    i = lax.broadcasted_iota(jnp.int32, (wide, wide), 0)
-    j = lax.broadcasted_iota(jnp.int32, (wide, wide), 1)
-    back_ref[...] = ((i + j == FP - 1 - (FP - wide)) & (i < FP // 2)).astype(F32).astype(BF16)
+    i = lax.broadcasted_iota(jnp.int32, (side, wide), 0)
+    j = lax.broadcasted_iota(jnp.int32, (side, wide), 1)
+    back_ref[...] = (i + j == wide - 1).astype(F32).astype(BF16)
 
 
 def one_hot(rows, index):
@@ -283,21 +283,21 @@
             odd_re = odd[:band]
             odd_im = odd[band:]
             rows = [(re, -odd_im), (im, odd_re), (re, odd_im), (im, -odd_re)]
-            rows = [jnp.concatenate(pair, axis=1) for pair in rows]
-            parts.append(jnp.concatenate(rows + [jnp.zeros((2 * LANES - 4 * band, pup), BF16)], axis=0))
+            parts.append(jnp.concatenate([jnp.concatenate(pair, axis=1) for pair in rows], axis=0))
         return parts
 
     def far_side(table, mid):
         mid_hi, mid_lo = mid
         hi, lo = table
-        return mm_t(hi, jnp.concatenate([mid_hi, mid_lo], axis=0)), mm_t(lo, mid_hi)
+        return mm_t(jnp.concatenate([mid_hi, mid_lo], axis=0), hi), mm_t(mid_hi, lo)
 
     def unfold(field, low):
-        field = field[:, : 2 * LANES] + field[:, 2 * LANES :] + low
-        field = jnp.concatenate([field, jnp.zeros((2 * LANES - side, 2 * LANES), F32)], axis=0).T
+        field = field[: 4 * band] + field[4 * band :] + low
         field = field * field
-        far_hi, far_lo = split2(field[2 * band : 3 * band] + field[3 * band : 4 * band])
-        return field[:band] + field[band : 2 * band], mm(jnp.concatenate([far_hi, far_lo], axis=0), back)
+        near = field[:band] + field[band : 2 * band]
+        near = jnp.concatenate([near, jnp.zeros((band, 2 * LANES - side), F32)], axis=1)
+        far_hi, far_lo = split2(field[2 * band : 3 * band] + field[3 * band :])
+        return near, mm(jnp.concatenate([far_hi, far_lo], axis=0), back)
 
     def finish(w, near, far, stat):
         far = far[:band] + far[band:]
@@ -368,8 +368,8 @@
     waves = wavelengths.shape[0] // (cols // cands)
     band = FP // rows
     holes = dark_hole.shape[0]
-    square = [jax.ShapeDtypeStruct((n, n), BF16) for n in (PUP // 2, 2 * LANES)]
-    flip, back = call(reversal_kernel, "reversals", square, [])
+    matrices = [jax.ShapeDtypeStruct(s, BF16) for s in ((PUP // 2, PUP // 2), (FP // 2, 2 * LANES))]
+    flip, back = call(reversal_kernel, "reversals", matrices, [])
     share, mask = call(
         pick_kernel, "pick", [(cols, 1, tile_rows), (band, FP)],
         [estimate, dark_hole.reshape(1, holes), flip],

time: 78.3 us -> 78 us (level)
  no operation moved by 1% of the time
where the time goes in v7:
time: 78 us; the launch traced here: 77.7 us
  blocking collectives  65.5 us (84%)
  Pallas kernels  10.5 us (13%)
  local copies, waits for them, and re-layouts  0.91 us (1%)
    all_to_all x6, blocking collectives, exchange(): return lax.all_to_all(x, axis, 0, 0)  65.5 us
    pallas_call x8, Pallas kernels, call(): pl.pallas_call(kernel, out_shape=[jax.ShapeDtypeStruct(s, F32) if isinsta...  10.5 us

profile of v7, /device:TPU:1, one launch (start us, length us, event | category | flops | bytes accessed | tf_op | source)
XLA Modules:
  0.0 77.7 jit_solution(15091892494022498393)
XLA Ops:
  0.6 0.0 copy-start.4
  0.6 0.0 copy-start.3
  0.6 0.0 slice-start.3
  0.7 0.0 slice-start.4
  0.7 0.6 copy-done.4
  1.3 0.2 copy-done.3
  1.6 1.0 %pick.1 = (f32[16,1,2048]{2,1,0:T(1,128)S(1)}, f32[48,384]{1,0:T(8,128)S(1)}) custom-call(f32[4,9216]{1,0:T(4,128)S(1)} %copy-done.3, s32[1,4096]{1,0:T(1,128)S(1)} %bitcast.7, bf16[128,128]{1,0:T(8,128)(2,1)S(1)} %get-tuple-element.14.after_ref.flip_ref), custom_call_target="tpu_custom_call" | custom-call | flops 20000000000 | bytes 1048576 | tf_op jit(solution)/shard_map/pick/pallas_call | solution.py:346
  2.5 14.5 %all_to_all.30.field_ref = f32[16,1,2048]{2,1,0:T(1,128)S(1)} all-to-all(f32[16,1,2048]{2,1,0:T(1,128)S(1)} %get-tuple-element.15), channel_id=1, replica_groups=mesh['rows'=8,'cols'=16] {'cols'}, dimensions={0} | all-to-all | bytes 262144 | tf_op jit(solution)/shard_map/all_to_all | solution.py:359
  17.0 0.0 slice-done.3
  17.0 0.0 slice-done.4
  17.0 0.0 slice-done.5
  17.1 0.0 slice-start.2
  17.1 0.8 %gradient.1 = f32[8,1,1152]{2,1,0:T(1,128)S(1)} custom-call(f32[16,1,2048]{2,1,0:T(1,128)S(1)} %all_to_all.30.field_ref, f32[2048,1152]{1,0:T(8,128)S(1)} %bitcast.5), custom_call_target="tpu_custom_call" | custom-call | flops 20000000000 | bytes 1048576 | tf_op jit(solution)/shard_map/gradient/pallas_call | solution.py:346
  17.9 11.9 %all_to_all.31.grad_ref = f32[8,1,1152]{2,1,0:T(1,128)S(1)} all-to-all(f32[8,1,1152]{2,1,0:T(1,128)S(1)} %gradient.1), channel_id=1, replica_groups=mesh['rows'=8,'cols'=16] {'rows'}, dimensions={0} | all-to-all | bytes 73728 | tf_op jit(solution)/shard_map/all_to_all | solution.py:359
  29.8 0.0 slice-done
  29.8 0.0 slice-done.1
  29.8 0.0 slice-done.2
  29.8 0.0 copy-start.5
  29.8 0.8 %modal.1 = f32[16,1,2304]{2,1,0:T(1,128)S(1)} custom-call(f32[8,1,1152]{2,1,0:T(1,128)S(1)} %all_to_all.31.grad_ref, f32[2304,1152]{1,0:T(8,128)S(1)} %bitcast.3), custom_call_target="tpu_custom_call" | custom-call | flops 20000000000 | bytes 1048576 | tf_op jit(solution)/shard_map/modal/pallas_call | solution.py:346
  30.6 9.8 %all_to_all.32.modal_ref = f32[16,1,2304]{2,1,0:T(1,128)S(1)} all-to-all(f32[16,1,2304]{2,1,0:T(1,128)S(1)} %modal.1), channel_id=1, replica_groups=mesh['rows'=8,'cols'=16] {'cols'}, dimensions={0} | all-to-all | bytes 294912 | tf_op jit(solution)/shard_map/all_to_all | solution.py:359
  40.4 0.0 copy-done.5
  40.4 2.0 %commands.1 = f32[8,1,6912]{2,1,0:T(1,128)S(1)} custom-call(f32[16,1,2304]{2,1,0:T(1,128)S(1)} %all_to_all.32.modal_ref, f32[2304]{0:T(1024)S(1)} %copy-done.5, f32[2304,1152]{1,0:T(8,128)S(1)} %bitcast.3), custom_call_target="tpu_custom_call" | custom-call | flops 20000000000 | bytes 1048576 | tf_op jit(solution)/shard_map/commands/pallas_call | solution.py:346
  42.4 10.6 %all_to_all.33.parts_ref = f32[8,1,6912]{2,1,0:T(1,128)S(1)} all-to-all(f32[8,1,6912]{2,1,0:T(1,128)S(1)} %commands.1), channel_id=1, replica_groups=mesh['rows'=8,'cols'=16] {'rows'}, dimensions={0} | all-to-all | bytes 442368 | tf_op jit(solution)/shard_map/all_to_all | solution.py:359
  53.0 0.0 copy-done.6
  53.0 0.0 copy-start.7
  53.0 0.6 gather.1
  53.6 9.3 %all_to_all.34.cmd_ref = f32[16,1,1152]{2,1,0:T(1,128)S(1)} all-to-all(f32[16,1,1152]{2,1,0:T(1,128)S(1)} %get-tuple-element.16), channel_id=1, replica_groups=mesh['rows'=8,'cols'=16] {'cols'}, dimensions={0} | all-to-all | bytes 147456 | tf_op jit(solution)/shard_map/all_to_all | solution.py:359
  62.9 0.0 copy-done
  62.9 0.0 copy-done.1
  63.0 4.5 %check.1 = (f32[6,48,384]{2,1,0:T(8,128)S(1)}, f32[8,1,128]{2,1,0:T(1,128)S(1)}, f32[8,1152]{1,0:T(8,128)}) custom-call(f32[16,1,1152]{2,1,0:T(1,128)S(1)} %all_to_all.34.cmd_ref, f32[2,96,256]{2,1,0:T(8,128)S(1)} %bitcast.6, f32[256,256]{1,0:T(8,128)S(1)} %copy-done, f32[256,256]{1,0:T(8,128)S(1)} %copy-done.1, f32[12]{0:T(128)S(1)} %copy-done.7, ...), custom_call_target="tpu_custom_call" | custom-call | flops 20000000000 | bytes 1048576 | tf_op jit(solution)/shard_map/check/pallas_call | solution.py:346
  67.5 9.3 %all_to_all.35.stat_ref = f32[8,1,128]{2,1,0:T(1,128)S(1)} all-to-all(f32[8,1,128]{2,1,0:T(1,128)S(1)} %get-tuple-element.21), channel_id=1, replica_groups=mesh['rows'=8,'cols'=16] {'rows'}, dimensions={0} | all-to-all | bytes 8192 | tf_op jit(solution)/shard_map/all_to_all | solution.py:359
  76.8 0.9 %scale.1 = (f32[6,48,384]{2,1,0:T(8,128)}, f32[1,6]{1,0:T(1,128)}) custom-call(f32[8,1,128]{2,1,0:T(1,128)S(1)} %all_to_all.35.stat_ref, f32[6,48,384]{2,1,0:T(8,128)S(1)} %get-tuple-element.22.int_ref), custom_call_target="tpu_custom_call" | custom-call | flops 20000000000 | bytes 1048576 | tf_op jit(solution)/shard_map/scale/pallas_call | solution.py:346
  (12 shorter events, 0.0 us)
Async XLA Ops:
  0.6 0.7 copy-start.4
  0.6 0.9 %copy-start.3 = (f32[4,9216]{1,0:T(4,128)S(1)}, f32[4,9216]{1,0:T(4,128)}, u32[]{:S(2)}) copy-start(f32[4,9216]{1,0:T(4,128)} %est_ref.1) | copy-start | bytes 442372
  0.6 16.4 %slice-start.3 = ((s8[9437184]{0:T(1024)(128)(4,1)}), s8[4194304]{0:T(1024)(128)(4,1)S(1)}, s32[]{:S(2)}) async-start(s8[9437184]{0:T(1024)(128)(4,1)} %bitcast.4), calls=%async_computation.9 | async-start | bytes 8388608
  0.7 16.4 %slice-start.4 = ((s8[9437184]{0:T(1024)(128)(4,1)}), s8[4194304]{0:T(1024)(128)(4,1)S(1)}, s32[]{:S(2)}) async-start(s8[9437184]{0:T(1024)(128)(4,1)} %bitcast.4), calls=%async_computation.10 | async-start | bytes 8388608
  1.6 15.5 %slice-start.5 = ((s8[9437184]{0:T(1024)(128)(4,1)}), s8[1048576]{0:T(1024)(128)(4,1)S(1)}, s32[]{:S(2)}) async-start(s8[9437184]{0:T(1024)(128)(4,1)} %bitcast.4), calls=%async_computation.11 | async-start | bytes 2097152
  1.6 28.2 %slice-start = ((s8[10616832]{0:T(1024)(128)(4,1)}), s8[4194304]{0:T(1024)(128)(4,1)S(1)}, s32[]{:S(2)}) async-start(s8[10616832]{0:T(1024)(128)(4,1)} %bitcast.2), calls=%async_computation.6 | async-start | bytes 8388608
  1.6 28.2 %slice-start.1 = ((s8[10616832]{0:T(1024)(128)(4,1)}), s8[4194304]{0:T(1024)(128)(4,1)S(1)}, s32[]{:S(2)}) async-start(s8[10616832]{0:T(1024)(128)(4,1)} %bitcast.2), calls=%async_computation.7 | async-start | bytes 8388608
  17.1 12.7 %slice-start.2 = ((s8[10616832]{0:T(1024)(128)(4,1)}), s8[2228224]{0:T(1024)(128)(4,1)S(1)}, s32[]{:S(2)}) async-start(s8[10616832]{0:T(1024)(128)(4,1)} %bitcast.2), calls=%async_computation.8 | async-start | bytes 4456448
  29.8 10.6 %copy-start.5 = (f32[2304]{0:T(1024)S(1)}, f32[2304]{0:T(1024)}, u32[]{:S(2)}) copy-start(f32[2304]{0:T(1024)} %eig_ref.1) | copy-start | bytes 27652
  40.4 12.6 %copy-start.6 = (s32[8]{0:T(128)S(1)}, s32[8]{0:T(128)}, u32[]{:S(2)}) copy-start(s32[8]{0:T(128)} %exp_ref.1) | copy-start | bytes 100
  53.0 9.9 %copy-start = (f32[256,256]{1,0:T(8,128)S(1)}, f32[256,256]{1,0:T(8,128)}, u32[]{:S(2)}) copy-start(f32[256,256]{1,0:T(8,128)} %aber_ref.1) | copy-start | bytes 786436
  53.0 9.9 %copy-start.1 = (f32[256,256]{1,0:T(8,128)S(1)}, f32[256,256]{1,0:T(8,128)}, u32[]{:S(2)}) copy-start(f32[256,256]{1,0:T(8,128)} %amp_ref.1) | copy-start | bytes 786436
  53.0 9.9 %copy-start.2 = (f32[2,256,96]{1,2,0:T(8,128)S(1)}, f32[2,256,96]{1,2,0:T(8,128)}, u32[]{:S(2)}) copy-start(f32[2,256,96]{1,2,0:T(8,128)} %param.19) | copy-start | bytes 589828
  53.0 9.9 %copy-start.7 = (f32[12]{0:T(128)S(1)}, f32[12]{0:T(128)}, u32[]{:S(2)}) copy-start(f32[12]{0:T(128)} %wave_ref.1) | copy-start | bytes 148
